TPU v7x, 128 devices: a whole 4x4x4 slice. The times are simulated.
128 devices in a mesh: region: 64 (over z, y, x_hi, core), obs: 2 (over x_lo).
Axes of the slice: x: 4 (x_hi: 2, x_lo: 2; x = x_hi * 2 + x_lo), y: 4, z: 4, core: 2. Of those that a mesh axis runs over, the one named last changes fastest.
Arguments:
- obs_anomaly: bfloat16 [2048, 2048, 128], P('region', 'obs'), may hold values from -1.5 to 1.5
- innovation: bfloat16 [2048, 2048], P('region', 'obs'), may hold values from -6 to 6
- obs_count: int32 [2048], P('region'), may hold values from 512 to 2048, as said below
- neighbour: int32 [2048, 5], P('region'), may hold values from 0 to 2047, as said below
- taper: float32 [2048, 5], P('region'), may hold values from 0.1 to 1
- param_anomaly: bfloat16 [2048, 1024, 128], P('region', 'obs'), may hold values from -6 to 6
- param_mean: float32 [2048, 1024], P('region', 'obs'), may hold values from -6 to 6
Outputs:
- analysis: bfloat16 [2048, 1024, 128], P('region', 'obs')
Inputs may be any that keep to these rules, and one draw needn't show every extreme that they name: `obs_count`: region 2048 counts: some region has all 2048 slots live. neighbour[g, 0] = g; every other entry differs from g cyclically by 1 to 32 regions.
All inputs are finite; a program needn't handle non-finite values.
Results may differ from a plain program's by a relative error of at most 0.013.
Values may be sent and summed in bfloat16 or wider, within the bound.
No kernel may reach another device: no remote copies, remote signals or barrier semaphores. Data moves between devices by JAX's collectives and lax.ppermute only.
A program may use at most 192 MiB of HBM per device.

v0:
```python
import jax
import jax.numpy as jnp
from jax import lax
from jax.sharding import PartitionSpec as P


def with_halo(array, sides, width):
    for axis, dim in sides:
        size, length = (lax.axis_size(axis), array.shape[dim])
        up = [(i, (i + 1) % size) for i in range(size)]
        down = [(j, i) for i, j in up]
        last = lax.slice_in_dim(array, length - width, length, axis=dim)
        leading = lax.slice_in_dim(array, 0, width, axis=dim)
        before = lax.ppermute(last, axis, up)
        after = lax.ppermute(leading, axis, down)
        array = jnp.concatenate([before, array, after], axis=dim)
    return array


def lower_inverse(lower):
    width = lower.shape[-1]
    rows = jnp.arange(width, dtype=jnp.int32)[:, None]
    cols = jnp.arange(width, dtype=jnp.int32)[None, :]
    diag = jnp.diagonal(lower, axis1=-2, axis2=-1)
    inverse = jnp.where(rows == cols, (1.0 / diag)[..., None, :], jnp.zeros((), jnp.float32))
    block = 1
    while block < width:
        row_block = rows // block
        col_block = cols // block
        keep = (row_block % 2 == 1) & (col_block == row_block - 1)
        corner = jnp.where(keep, lower, jnp.zeros((), jnp.float32))
        inner = jnp.einsum("bij,bjk->bik", corner, inverse, precision=lax.Precision.HIGHEST)
        inverse = inverse - jnp.einsum(
            "bij,bjk->bik", inverse, inner, precision=lax.Precision.HIGHEST
        )
        block = block * 2
    return inverse


def solve_region(local_gram, local_proj):
    width = local_gram.shape[-1]
    eye = jnp.eye(width, dtype=jnp.float32)
    precision_mat = (width - 1.0) * eye + local_gram
    lower = jnp.linalg.cholesky(precision_mat)
    inverse_lower = lower_inverse(lower)
    step_one = jnp.einsum("bij,bj->bi", inverse_lower, local_proj, precision=lax.Precision.HIGHEST)
    mean_weight = jnp.einsum("bji,bj->bi", inverse_lower, step_one, precision=lax.Precision.HIGHEST)
    spread = jnp.sqrt(width - 1.0) * jnp.swapaxes(inverse_lower, -1, -2)
    return (mean_weight[..., None] + spread).astype(jnp.bfloat16)


def body(obs_anomaly, innovation, obs_count, neighbour, taper, param_anomaly, param_mean):
    regions = obs_anomaly.shape[0]
    slot_count = obs_anomaly.shape[1]
    total = regions * lax.axis_size("region")
    first = lax.axis_index("region") * regions
    slots = lax.axis_index("obs") * slot_count + jnp.arange(slot_count, dtype=jnp.int32)
    live = slots[None, :] < obs_count[:, None]
    masked_y = jnp.where(live[..., None], obs_anomaly, jnp.zeros((), jnp.bfloat16))
    masked_d = jnp.where(live, innovation, jnp.zeros((), jnp.bfloat16))
    position = (neighbour - first + regions) % total
    grams = jnp.einsum("roi,roj->rij", masked_y, masked_y, preferred_element_type=jnp.float32)
    projs = jnp.einsum("roi,ro->ri", masked_y, masked_d, preferred_element_type=jnp.float32)
    wide_g, wide_p = (
        with_halo(grams.astype(jnp.bfloat16), (("region", 0),), regions).astype(grams.dtype),
        with_halo(projs.astype(jnp.bfloat16), (("region", 0),), regions).astype(projs.dtype),
    )
    local_gram = jnp.einsum(
        "rk,rkij->rij", taper, wide_g[position], precision=lax.Precision.HIGHEST
    )
    local_proj = jnp.einsum("rk,rki->ri", taper, wide_p[position], precision=lax.Precision.HIGHEST)
    summed_gram, summed_proj = (
        lax.psum(local_gram.astype(jnp.bfloat16), "obs").astype(jnp.float32),
        lax.psum(local_proj.astype(jnp.bfloat16), "obs").astype(jnp.float32),
    )
    transform = solve_region(summed_gram, summed_proj)
    moved = jnp.einsum("rpk,rkj->rpj", param_anomaly, transform, preferred_element_type=jnp.float32)
    return (param_mean[..., None] + moved).astype(jnp.bfloat16)


def solution(mesh):
    in_specs = (
        P("region", "obs", None),
        P("region", "obs"),
        P("region"),
        P("region", None),
        P("region", None),
        P("region", "obs", None),
        P("region", "obs"),
    )
    out_specs = P("region", "obs", None)
    return jax.shard_map(body, mesh=mesh, in_specs=in_specs, out_specs=out_specs, check_vma=False)
```

profile of v0, /device:TPU:0, one launch (start us, length us, event | category | flops | bytes accessed | tf_op | source)
XLA Modules:
  0.0 621.2 jit_solution(6216769820537432038)
XLA Ops:
  8.4 9.0 %fusion = f32[32,1,128]{2,1,0:T(1,128)S(1)} fusion(bf16[32,1024,128]{2,1,0:T(8,128)(2,1)} %param.7, pred[32,1024]{1,0:T(8,128)(4,1)S(1)} %broadcast_compare_fusion, bf16[32,1024,1]{1,0,2:T(8,128)(2,1)S(1)} %select_bitcast_fusion), kind=kOutput, calls=%fused_computation.6 | convolution fusion | flops 12582912 | bytes 8503296 | tf_op jit(solution)/shard_map/roi,ro->ri/dot_general | solution.py:63
  17.4 8.5 %collective-permute-start.3 = (bf16[32,128]{1,0:T(8,128)(2,1)S(1)}, bf16[32,128]{1,0:T(8,128)(2,1)S(1)}, u32[]{:S(2)}, u32[]{:S(2)}) collective-permute-start(bf16[32,128]{1,0:T(8,128)(2,1)S(1)} %convert_element_type.31), channel_id=1, source_target_pairs={{2,0},{4,2},{6,4},{8,6},{10,8},{12,10},{14,12},{16,14},{18,16},{20... | collective-permute-start | bytes 24584 | tf_op jit(solution)/shard_map/ppermute | solution.py:15
  26.0 6.6 %broadcast_select_fusion.10 = bf16[32,1024,128]{2,1,0:T(8,128)(2,1)} fusion(bf16[32,1024,128]{2,1,0:T(8,128)(2,1)S(1)} %bitcast.90, pred[32,1024]{1,0:T(8,128)(4,1)S(1)} %broadcast_compare_fusion), kind=kLoop, calls=%fused_computation.5.clone.1.clone.clone.clone.2 | loop fusion | flops 4194304 | bytes 16809984 | tf_op jit(solution)/shard_map/roi,roj->rij/dot_general | solution.py:62
  32.6 8.3 %fusion.28 = bf16[32,128,128]{2,1,0:T(8,128)(2,1)S(1)} fusion(bf16[32,1024,128]{2,1,0:T(8,128)(2,1)} %broadcast_select_fusion.10), kind=kOutput, calls=%fused_computation.47 | convolution fusion | flops 1074266112 | bytes 9437184 | tf_op jit(solution)/shard_map/roi,roj->rij/dot_general | solution.py:62
  40.9 7.5 %collective-permute-start.1 = (bf16[32,128,128]{2,1,0:T(8,128)(2,1)S(1)}, bf16[32,128,128]{2,1,0:T(8,128)(2,1)S(1)}, u32[]{:S(2)}, u32[]{:S(2)}) collective-permute-start(bf16[32,128,128]{2,1,0:T(8,128)(2,1)S(1)} %fusion.28), channel_id=1, source_target_pairs={{2,0},{4,2},{6,4},{8,6},{10,8},{12,10},{14,12},{16,14},{18,16},{20... | collective-permute-start | bytes 3145736 | tf_op jit(solution)/shard_map/ppermute | solution.py:15
  49.5 14.9 %collective-permute-done.1 = bf16[32,128,128]{2,1,0:T(8,128)(2,1)S(1)} collective-permute-done((bf16[32,128,128]{2,1,0:T(8,128)(2,1)S(1)}, bf16[32,128,128]{2,1,0:T(8,128)(2,1)S(1)}, u32[]{:S(2)}, u32[]{:S(2)}) %collective-permute-start.1) | collective-permute-done | bytes 1048608 | tf_op jit(solution)/shard_map/ppermute | solution.py:15
  65.3 3.6 collective-permute-done
  71.0 7.7 %gather_fusion = bf16[160,128,128]{2,1,0:T(8,128)(2,1)} fusion(bf16[96,128,128]{2,1,0:T(8,128)(2,1)S(1)} %pad_maximum_fusion, s32[1024]{0:T(1024)S(1)} %pad_clamp_fusion), kind=kCustom, calls=%fused_computation | custom fusion | bytes 10486400 | tf_op jit(solution)/shard_map/gather | solution.py:69
  78.7 4.1 multiply_reduce_fusion
  85.7 5.2 psum.15
  90.9 38.0 %all-reduce.2.cloned.1.call-done = bf16[32,128,128]{1,2,0:T(8,128)(2,1)} async-done(((bf16[32,128,128]{1,2,0:T(8,128)(2,1)}), bf16[32,128,128]{1,2,0:T(8,128)(2,1)}) %all-reduce.2.cloned.1.call-update) | async-done | bytes 1048592 | tf_op jit(solution)/shard_map/psum | solution.py:73
  132.2 3.3 fusion.12
  135.5 375.8 %custom-call.4 = f32[32,128,128]{2,1,0:T(8,128)S(1)} custom-call(f32[32,128,128]{2,1,0:T(8,128)} %fusion.12), custom_call_target="Cholesky" | custom-call | tf_op jit(solution)/shard_map/jit(cholesky)/cholesky | solution.py:44
  514.5 4.7 copy.43
  523.4 3.6 fusion.5
  527.1 3.3 copy.46
  530.4 4.1 fusion.23
  534.4 3.9 fusion.26
  541.3 3.9 fusion.21
  545.3 3.6 fusion.93
  551.9 3.9 fusion.19
  555.8 3.6 fusion.94
  559.5 3.0 copy.49
  562.5 3.9 fusion.17
  566.5 3.6 fusion.95
  573.0 3.9 fusion.15
  577.0 3.5 fusion.96
  582.8 3.6 fusion.97
  588.3 3.2 copy.52
  591.5 3.5 convolution_bitcast_fusion
  596.9 10.8 %fusion.2 = bf16[32,512,128]{1,2,0:T(8,128)(2,1)} fusion(f32[32,512]{1,0:T(8,128)S(1)} %copy-done.13, bf16[32,512,128]{2,1,0:T(8,128)(2,1)} %param.12, f32[32,128,128]{1,2,0:T(8,128)} %copy.52, f32[32,128,128]{1,2,0:T(8,128)} %copy.51, f32[32,128,128]{1,2,0:T(8,128)} %copy.50, f32[32,128,128]{1,2,0:T(8,128)} %copy.49, f32[32,128,128]{1,2,0:T(8,128)} %copy.48, ...), kind=kOutput, calls=%fused_computation.8 | convolution fusion | flops 546832384 | bytes 23183360 | tf_op jit(solution)/shard_map/rpk,rkj->rpj/dot_general | solution.py:77
  607.7 6.4 %copy.54 = bf16[32,512,128]{2,1,0:T(8,128)(2,1)} copy(bf16[32,512,128]{1,2,0:T(8,128)(2,1)} %fusion.2) | data formatting | bytes 8388608 | tf_op jit(solution)/shard_map/convert_element_type | solution.py:78
  (102 shorter events, 34.3 us)
Async XLA Ops:
  6.5 122.3 %all-reduce.2.cloned.1.call-start = ((), (), s32[]{:S(2)}) async-start(), calls=%async_computation | async-start | bytes 2097152 | tf_op jit(solution)/shard_map/psum | solution.py:73
  7.3 18.7 %slice-start = ((s8[8388608]{0:T(1024)(128)(4,1)}), s8[4194304]{0:T(1024)(128)(4,1)S(1)}, s32[]{:S(2)}) async-start(s8[8388608]{0:T(1024)(128)(4,1)} %bitcast.89), calls=%async_computation.1 | async-start | bytes 8388608
  8.4 17.6 %slice-start.1 = ((s8[8388608]{0:T(1024)(128)(4,1)}), s8[4194304]{0:T(1024)(128)(4,1)S(1)}, s32[]{:S(2)}) async-start(s8[8388608]{0:T(1024)(128)(4,1)} %bitcast.89), calls=%async_computation.2 | async-start | bytes 8388608
  17.4 67.2 %collective-permute-start.3 = (bf16[32,128]{1,0:T(8,128)(2,1)S(1)}, bf16[32,128]{1,0:T(8,128)(2,1)S(1)}, u32[]{:S(2)}, u32[]{:S(2)}) collective-permute-start(bf16[32,128]{1,0:T(8,128)(2,1)S(1)} %convert_element_type.31), channel_id=1, source_target_pairs={{2,0},{4,2},{6,4},{8,6},{10,8},{12,10},{14,12},{16,14},{18,16},{20... | collective-permute-start | bytes 24584 | tf_op jit(solution)/shard_map/ppermute | solution.py:15
  25.9 58.7 %collective-permute-start.2 = (bf16[32,128]{1,0:T(8,128)(2,1)S(1)}, bf16[32,128]{1,0:T(8,128)(2,1)S(1)}, u32[]{:S(2)}, u32[]{:S(2)}) collective-permute-start(bf16[32,128]{1,0:T(8,128)(2,1)S(1)} %convert_element_type.31), channel_id=1, source_target_pairs={{0,2},{2,4},{4,6},{6,8},{8,10},{10,12},{12,14},{14,16},{16,18},{18... | collective-permute-start | bytes 24584 | tf_op jit(solution)/shard_map/ppermute | solution.py:14
  32.6 16.0 %copy-start.15 = (s32[32,5]{0,1:T(8,128)S(1)}, s32[32,5]{0,1:T(8,128)}, u32[]{:S(2)}) copy-start(s32[32,5]{0,1:T(8,128)} %param.10) | copy-start | bytes 1924
  32.6 16.4 %copy-start.14 = (f32[32,5]{0,1:T(8,128)S(1)}, f32[32,5]{0,1:T(8,128)}, u32[]{:S(2)}) copy-start(f32[32,5]{0,1:T(8,128)} %param.11) | copy-start | bytes 1924
  40.9 23.5 %copy-start.10 = (bf16[32,128,128]{2,1,0:T(8,128)(2,1)}, bf16[32,128,128]{2,1,0:T(8,128)(2,1)S(1)}, u32[]{:S(2)}) copy-start(bf16[32,128,128]{2,1,0:T(8,128)(2,1)S(1)} %fusion.28) | copy-start | bytes 3145732
  40.9 23.4 %collective-permute-start.1 = (bf16[32,128,128]{2,1,0:T(8,128)(2,1)S(1)}, bf16[32,128,128]{2,1,0:T(8,128)(2,1)S(1)}, u32[]{:S(2)}, u32[]{:S(2)}) collective-permute-start(bf16[32,128,128]{2,1,0:T(8,128)(2,1)S(1)} %fusion.28), channel_id=1, source_target_pairs={{2,0},{4,2},{6,4},{8,6},{10,8},{12,10},{14,12},{16,14},{18,16},{20... | collective-permute-start | bytes 3145736 | tf_op jit(solution)/shard_map/ppermute | solution.py:15
  48.4 20.5 %collective-permute-start = (bf16[32,128,128]{2,1,0:T(8,128)(2,1)S(1)}, bf16[32,128,128]{2,1,0:T(8,128)(2,1)}, u32[]{:S(2)}, u32[]{:S(2)}) collective-permute-start(bf16[32,128,128]{2,1,0:T(8,128)(2,1)S(1)} %fusion.28), channel_id=1, source_target_pairs={{0,2},{2,4},{4,6},{6,8},{8,10},{10,12},{12,14},{14,16},{16,18},{18... | collective-permute-start | bytes 3145736 | tf_op jit(solution)/shard_map/ppermute | solution.py:14
  64.4 1.0 copy-start.12
  130.3 1.8 copy-start.11
  511.3 1.3 copy-start.8
  530.3 4.1 copy-start.3
  541.3 3.9 copy-start.4
  551.9 3.9 copy-start.5
  562.5 4.0 copy-start.6
  573.0 3.9 copy-start.7
  580.5 2.3 copy-start
  582.8 3.6 copy-start.9
  588.3 3.2 copy-start.1
  591.5 3.5 copy-start.2
  595.0 2.0 copy-start.13
Sparse Core Ops, SparseCore 0:
  84.3 44.5 all-reduce.1
where the time goes:
time: 631 us; the launch traced here: 621 us
  other arithmetic  398 us (63%)
  matrix products  83.8 us (13%)
  waiting for transfers between devices  56.5 us (9%)
  local copies, waits for them, and re-layouts  47.4 us (8%)
  starting transfers between devices  16.1 us (3%)
  between operations  14.2 us (2%)
    another operation x3, other arithmetic, solve_region(): lower = jnp.linalg.cholesky(precision_mat)  376 us
    psum x1, waiting for transfers between devices, body(): lax.psum(local_gram.astype(jnp.bfloat16), 'obs').astype(jnp.float32)  38 us
    dot_general x7, matrix products, lower_inverse(): jnp.einsum('bij,bjk->bik', inverse, inner, precision=lax.Precision.HIGHEST)  25.6 us
    dot_general x7, matrix products, lower_inverse(): jnp.einsum('bij,bjk->bik', corner, inverse, precision=lax.Precision.HIGHEST)  24.4 us
    dot_general x7, local copies, waits for them, and re-layouts, lower_inverse(): jnp.einsum('bij,bjk->bik', inverse, inner, precision=lax.Precision.HIGHEST)  20.2 us
    ppermute x2, starting transfers between devices, with_halo(): after = lax.ppermute(leading, axis, down)  16.1 us
    ppermute x2, waiting for transfers between devices, with_halo(): after = lax.ppermute(leading, axis, down)  14.9 us
  transfers between devices with their start and end apart: 5, of which 3 were waited for; matrix products, arithmetic and copies ran while one was open for 5% of the time, Pallas kernels for 0%

commit v1 on v0

v1 whole, which is shorter than its diff:
```python
import functools

import jax
import jax.numpy as jnp
from jax import lax
from jax.experimental import pallas as pl
from jax.experimental.pallas import tpu as pltpu
from jax.sharding import PartitionSpec as P

N = 128
HALF = 64
BLK = 16
GRP = 16
F32 = jnp.float32
BF16 = jnp.bfloat16


def iota(shape, dim):
    return lax.broadcasted_iota(jnp.int32, shape, dim)


def pack(gram):
    top, bottom = gram[:HALF], pltpu.roll(gram[HALF:], HALF, 1)
    return jnp.where(iota((HALF, N), 1) >= iota((HALF, N), 0), top, bottom)


def gram_kernel(step, count_ref, y_ref, d_ref, out_ref):
    slots = y_ref.shape[1]
    base = pl.program_id(0) * step
    total = d_ref.shape[0]
    rows = lax.broadcasted_iota(jnp.int16, (slots, N), 0)
    drows = iota((BLK, N), 0)
    for s in range(step):
        r = base + s
        live = jnp.clip(count_ref[r], 0, slots).astype(jnp.int16)
        y = jnp.where(rows < live, y_ref[s], jnp.zeros((), BF16))
        start = pl.multiple_of((r // BLK) * BLK, BLK)
        lhs = jnp.concatenate([y.T, d_ref[pl.ds(start, BLK), :]], axis=0)
        full = jnp.dot(lhs, y, preferred_element_type=F32)
        gram = full[:N]
        proj = jnp.sum(jnp.where(drows == r - start, full[N:], 0.0), axis=0, keepdims=True)
        diag = jnp.sum(
            jnp.where(iota((HALF, N), 0) + HALF == iota((HALF, N), 1), gram[HALF:], 0.0),
            axis=0, keepdims=True,
        )
        out_ref[r] = pack(gram).astype(BF16)
        at = iota((total, N), 0) == r
        extra_d, extra_p = out_ref[total, 0:total], out_ref[total, total:2 * total]
        out_ref[total, 0:total] = jnp.where(at, diag, extra_d.astype(F32)).astype(BF16)
        out_ref[total, total:2 * total] = jnp.where(at, proj, extra_p.astype(F32)).astype(BF16)


def grams(live, obs_anomaly, innovation, step=4):
    regions, slots, _ = obs_anomaly.shape
    return pl.pallas_call(
        functools.partial(gram_kernel, step),
        out_shape=jax.ShapeDtypeStruct((regions + 1, HALF, N), BF16),
        grid_spec=pltpu.PrefetchScalarGridSpec(
            num_scalar_prefetch=1,
            grid=(regions // step,),
            in_specs=[
                pl.BlockSpec((step, slots, N), lambda i, c: (i, 0, 0)),
                pl.BlockSpec((regions, slots), lambda i, c: (0, 0)),
            ],
            out_specs=pl.BlockSpec((regions + 1, HALF, N), lambda i, c: (0, 0, 0)),
        ),
        compiler_params=pltpu.CompilerParams(vmem_limit_bytes=48 << 20),
        name="grams",
    )(live, obs_anomaly, innovation)


def split(x):
    high = x.astype(BF16)
    return high, (x - high.astype(F32)).astype(BF16)


def expand(pair_packed, diags, mat_ref, row_a, row_b):
    la, lb = pair_packed
    i, j = iota((HALF, N), 0), iota((HALF, N), 1)
    turned = jnp.concatenate([la, lb], axis=0).T
    top, bottom = turned[:HALF], turned[HALF:]
    top_r, bottom_r = pltpu.roll(top, HALF, 1), pltpu.roll(bottom, HALF, 1)
    ridge = jnp.where(i == j, N - 1.0, 0.0)
    for row, lp, tt, tl, tr, dg in (
        (row_a, la, top, bottom, top_r, diags[0]), (row_b, lb, top_r, bottom_r, top, diags[1]),
    ):
        mat_ref[pl.ds(row, HALF), :] = jnp.where(i <= j, lp, tt) + ridge
        corner = jnp.where(i + HALF > j, pltpu.roll(lp, HALF, 1), tr)
        corner = jnp.where(i + HALF == j, dg + (N - 1.0), corner)
        mat_ref[pl.ds(row + HALF, HALF), :] = jnp.where(j < HALF, tl, corner)


def panel(mat_ref, z_ref, proj, mean, first, kb, last):
    lane = iota((GRP, N), 1)
    rows = [mat_ref[pl.ds(first * N + kb + i, GRP, stride=N), :] for i in range(BLK)]
    done = []
    for i in range(BLK):
        c = kb + i
        pivot = rows[i][:, c:c + 1]
        scale = lax.rsqrt(pivot)
        r = jnp.where(lane == c, 1.0, rows[i]) * scale
        done.append(jnp.where((lane > c) & (lane < kb + BLK), 0.0, r))
        for j in range(i + 1, BLK):
            factor = rows[i][:, kb + j:kb + j + 1] * scale
            rows[j] = jnp.where(lane == c, 0.0, rows[j]) - factor * r
        w = jnp.where(lane <= c, r, 0.0)
        mat_ref[pl.ds(first * N + c, GRP, stride=N), :] = w
        mean = mean + jnp.sum(w * proj, axis=1, keepdims=True) * w
    if not last:
        for j in range(BLK):
            z = done[j][:, kb + j:kb + j + 1] * done[j]
            for i in range(j + 1, BLK):
                z = z + done[i][:, kb + j:kb + j + 1] * done[i]
            z_ref[pl.ds(first * BLK + j, GRP, stride=BLK), :] = z
    return mean


def update(mat_ref, z_ref, m, kb):
    n = N - kb - BLK
    start = pl.multiple_of(m * N + kb + BLK, BLK)
    mat = mat_ref[pl.ds(start, n), :]
    high, low = split(mat)
    zh, zl = split(z_ref[pl.ds(pl.multiple_of(m * BLK, BLK), BLK), :])
    above, below = jnp.zeros((kb, N), BF16), jnp.zeros((n, N), BF16)

    def place(z):
        return jnp.concatenate([p for p in (above, z, below) if p.shape[0]], axis=0)

    bh, bl = place(zh), place(zl)
    change = jnp.dot(
        jnp.concatenate([high, low], axis=1), jnp.concatenate([bh, bh], axis=0),
        preferred_element_type=F32,
    ) + jnp.dot(high, bl, preferred_element_type=F32)
    lane = iota((n, N), 1)
    kept = jnp.where((lane >= kb) & (lane < kb + BLK), 0.0, mat)
    mat_ref[pl.ds(start, n), :] = kept - change


def solve_kernel(idx_ref, taper_ref, idxv_ref, taperv_ref, own_ref, near_ref, far_ref, out_ref,
                 wide_ref, mat_ref, z_ref, diag_ref, mean_ref, sems):
    regions = idxv_ref.shape[0]
    nb = idxv_ref.shape[1]
    copies = [
        pltpu.make_async_copy(src.at[pl.ds(0, regions)], wide_ref.at[pl.ds(s * regions, regions)], sems.at[s])
        for s, src in enumerate((own_ref, near_ref, far_ref))
    ] + [
        pltpu.make_async_copy(src.at[regions], wide_ref.at[3 * regions + s], sems.at[3 + s])
        for s, src in enumerate((own_ref, near_ref, far_ref))
    ]
    for c in copies:
        c.start()
    for c in copies:
        c.wait()
    tails = [wide_ref[3 * regions + s].astype(F32) for s in range(3)]
    sel_lane = iota((regions, 3 * regions), 1)
    weights = jnp.zeros((regions, 3 * regions), F32)
    for k in range(nb):
        weights = weights + jnp.where(sel_lane == idxv_ref[:, k:k + 1], taperv_ref[:, k:k + 1], 0.0)
    diag_all = jnp.concatenate([t[:regions] for t in tails], axis=0)
    proj_all = jnp.concatenate([t[regions:2 * regions] for t in tails], axis=0)
    diag_ref[...] = jnp.dot(weights, diag_all, precision=lax.Precision.HIGHEST, preferred_element_type=F32)
    proj = jnp.dot(weights, proj_all, precision=lax.Precision.HIGHEST, preferred_element_type=F32)

    def combine(pair, _):
        packed = []
        for q in range(2):
            r = 2 * pair + q
            acc = None
            for k in range(nb):
                term = taper_ref[r * nb + k] * wide_ref[idx_ref[r * nb + k]].astype(F32)
                acc = term if acc is None else acc + term
            packed.append(acc)
        row = pl.multiple_of(2 * pair * N, N)
        expand(packed, [diag_ref[pl.ds(2 * pair + q, 1), :] for q in range(2)], mat_ref, row, row + N)
        return 0

    lax.fori_loop(0, regions // 2, combine, 0)
    groups = regions // GRP
    means = [jnp.zeros((GRP, N), F32) for _ in range(groups)]
    for kb in range(0, N, BLK):
        last = kb + BLK == N
        for g in range(groups):
            means[g] = panel(mat_ref, z_ref, proj[g * GRP:(g + 1) * GRP], means[g], g * GRP, kb, last)
        if not last:
            def many(t, _):
                for u in range(8):
                    update(mat_ref, z_ref, t * 8 + u, kb)
                return 0

            lax.fori_loop(0, regions // 8, many, 0)
    mean_ref[...] = jnp.concatenate(means, axis=0)

    def finish(m, _):
        w = mat_ref[pl.ds(pl.multiple_of(m * N, N), N), :]
        out_ref[m] = (jnp.sqrt(jnp.float32(N - 1)) * w + mean_ref[pl.ds(m, 1), :]).astype(BF16)
        return 0

    lax.fori_loop(0, regions, finish, 0, unroll=2)


def solve(idx, taper, own, near, far):
    regions, nb = idx.shape
    hbm = pl.BlockSpec(memory_space=pl.ANY)
    smem = pl.BlockSpec(memory_space=pltpu.SMEM)
    vmem = pl.BlockSpec(memory_space=pltpu.VMEM)
    return pl.pallas_call(
        solve_kernel,
        out_shape=jax.ShapeDtypeStruct((regions, N, N), BF16),
        in_specs=[smem, smem, vmem, vmem, hbm, hbm, hbm],
        out_specs=vmem,
        scratch_shapes=[
            pltpu.VMEM((3 * regions + 3, HALF, N), BF16),
            pltpu.VMEM((regions * N, N), F32),
            pltpu.VMEM((regions * BLK, N), F32),
            pltpu.VMEM((regions, N), F32),
            pltpu.VMEM((regions, N), F32),
            pltpu.SemaphoreType.DMA((6,)),
        ],
        compiler_params=pltpu.CompilerParams(vmem_limit_bytes=48 << 20),
        name="solve",
    )(idx.reshape(-1), taper.reshape(-1), idx, taper, own, near, far)


def apply_kernel(step, mean_ref, turned_ref, param_ref, out_ref, column_ref):
    regions = mean_ref.shape[0]

    @pl.when(pl.program_id(0) == 0)
    def _():
        rest = mean_ref[...]
        pieces = []
        for _ in range(3):
            high = rest.astype(BF16).astype(F32)
            pieces.append(high)
            rest = rest - high
        pieces.append(jnp.zeros((N - 3 * regions, rest.shape[1]), F32))
        column_ref[...] = jnp.concatenate(pieces, axis=0).T.astype(BF16)

    lane = iota((N, N), 1)
    for s in range(step):
        r = pl.program_id(0) * step + s
        pick = ((lane == r) | (lane == regions + r) | (lane == 2 * regions + r)).astype(F32).astype(BF16)
        left = jnp.concatenate([param_ref[s], column_ref[...]], axis=1)
        right = jnp.concatenate([turned_ref[s], pick], axis=1)
        moved = lax.dot_general(left, right, (((1,), (1,)), ((), ())), preferred_element_type=F32)
        out_ref[s] = moved.astype(BF16)


def apply(param_mean, turned, param_anomaly, step=4):
    regions, params, _ = param_anomaly.shape
    return pl.pallas_call(
        functools.partial(apply_kernel, step),
        out_shape=jax.ShapeDtypeStruct(param_anomaly.shape, BF16),
        grid=(regions // step,),
        in_specs=[
            pl.BlockSpec((regions, params), lambda i: (0, 0)),
            pl.BlockSpec((step, N, N), lambda i: (i, 0, 0)),
            pl.BlockSpec((step, params, N), lambda i: (i, 0, 0)),
        ],
        out_specs=pl.BlockSpec((step, params, N), lambda i: (i, 0, 0)),
        scratch_shapes=[pltpu.VMEM((params, N), BF16)],
        compiler_params=pltpu.CompilerParams(vmem_limit_bytes=48 << 20),
        name="apply",
    )(param_mean, turned, param_anomaly)


def body(obs_anomaly, innovation, obs_count, neighbour, taper, param_anomaly, param_mean):
    regions, slots = obs_anomaly.shape[:2]
    size, half = lax.axis_size("region"), lax.axis_size("obs")
    total = regions * size
    here, part = lax.axis_index("region"), lax.axis_index("obs")
    devices = [(r, o) for r in range(size) for o in range(half)]

    def swap(x, other):
        line = [(r * half + o, (lambda a: (a[0] % size) * half + a[1])(other(r, o))) for r, o in devices]
        return lax.ppermute(x, ("region", "obs"), line)

    packed = grams(obs_count - part * slots, obs_anomaly, innovation)
    partner = swap(packed, lambda r, o: (r, 1 - o))
    own = (packed.astype(F32) + partner.astype(F32)).astype(BF16)
    far = swap(own, lambda r, o: (r + 1 if r % 2 else r - 1, 1 - o))
    near = swap(own, lambda r, o: (r ^ 1, o))
    place = (neighbour - here * regions + regions) % total
    even = here % 2 == 0
    before, after = jnp.where(even, 2, 1), jnp.where(even, 1, 2)
    slot = jnp.where(place < regions, before, jnp.where(place < 2 * regions, 0, after))
    idx = (slot * regions + place % regions).astype(jnp.int32)
    turned = solve(idx, taper, own, near, far)
    return apply(param_mean, turned, param_anomaly)


def solution(mesh):
    specs = (
        P("region", "obs", None), P("region", "obs"), P("region"), P("region", None),
        P("region", None), P("region", "obs", None), P("region", "obs"),
    )
    return jax.shard_map(body, mesh=mesh, in_specs=specs, out_specs=P("region", "obs", None), check_vma=False)
```

time: 631 us -> 109 us (0.17); the launches traced: 621 us -> 108 us
  other arithmetic: 398 us -> 0.87 us
  matrix products: 83.8 us -> 0 us
  Pallas kernels: 0 us -> 71.9 us
  local copies, waits for them, and re-layouts: 47.4 us -> 3.42 us
  waiting for transfers between devices: 56.5 us -> 22.9 us
  between operations: 14.2 us -> 0.07 us
  starting transfers between devices: 16.1 us -> 9.27 us
    another operation x3 -> x0, other arithmetic: 376 us -> none  [solve_region(): lower = jnp.linalg.cholesky(precision_mat)]
    dot_general x20 -> x0, matrix products: 83.8 us -> none  [the longest x7 25.6 us: lower_inverse(): jnp.einsum('bij,bjk->bik', inverse, inner, precision=lax.Precision.HIGHEST)]
    pallas_call x0 -> x3, Pallas kernels: none -> 71.9 us  [the longest x1 57.7 us: solve(): pl.pallas_call(solve_kernel, out_shape=jax.ShapeDtypeStruct((regions, N,...]
    psum x1 -> x0, waiting for transfers between devices: 38 us -> none  [body(): lax.psum(local_gram.astype(jnp.bfloat16), 'obs').astype(jnp.float32)]
    dot_general x8 -> x0, local copies, waits for them, and re-layouts: 21.5 us -> none  [the longest x7 20.2 us: lower_inverse(): jnp.einsum('bij,bjk->bik', inverse, inner, precision=lax.Precision.HIGHEST)]
    gather x4 -> x0, local copies, waits for them, and re-layouts: 10.3 us -> none  [the longest x1 7.72 us: body(): wide_g[position]]
    ppermute x4 -> x3, starting transfers between devices: 16.1 us -> 9.27 us  [swap(): return lax.ppermute(x, ('region', 'obs'), line)]
    dot_general x1 -> x0, other arithmetic: 6.62 us -> none  [body(): jnp.einsum('roi,roj->rij', masked_y, masked_y, preferred_element_type=jnp...]
  transfers between devices with their start and end apart: 5 -> 3, of which waited for: 3 -> 2; matrix products, arithmetic and copies ran while one was open for 5% -> 0% of each run, Pallas kernels for 0% -> 0%
where the time goes in v1:
time: 109 us; the launch traced here: 108 us
  Pallas kernels  71.9 us (66%)
  waiting for transfers between devices  22.9 us (21%)
  starting transfers between devices  9.27 us (9%)
  local copies, waits for them, and re-layouts  3.42 us (3%)
    pallas_call x1, Pallas kernels, solve(): pl.pallas_call(solve_kernel, out_shape=jax.ShapeDtypeStruct((regions, N,...  57.7 us
    ppermute x3, waiting for transfers between devices, swap(): return lax.ppermute(x, ('region', 'obs'), line)  22.9 us
    ppermute x3, starting transfers between devices, swap(): return lax.ppermute(x, ('region', 'obs'), line)  9.27 us
    pallas_call x1, Pallas kernels, grams(): pl.pallas_call(functools.partial(gram_kernel, step), out_shape=jax.ShapeD...  8.74 us
    pallas_call x1, Pallas kernels, apply(): pl.pallas_call(functools.partial(apply_kernel, step), out_shape=jax.Shape...  5.49 us
    unnamed x12, local copies, waits for them, and re-layouts  3.21 us
  transfers between devices with their start and end apart: 3, of which 2 were waited for; matrix products, arithmetic and copies ran while one was open for 0% of the time, Pallas kernels for 0%

profile of v1, /device:TPU:0, one launch (start us, length us, event | category | flops | bytes accessed | tf_op | source)
XLA Modules:
  0.0 108.4 jit_solution(5303376336862885348)
XLA Ops:
  0.0 0.7 broadcast_subtract_fusion.count_ref
  0.7 0.0 copy-start.1
  0.7 0.8 copy-done.1
  1.5 0.0 copy-start.3
  1.5 0.0 copy-start.4
  1.5 8.7 %grams.1 = bf16[33,64,128]{2,1,0:T(8,128)(2,1)S(1)} custom-call(s32[32]{0:T(128)S(1)} %broadcast_subtract_fusion.count_ref, bf16[32,1024,128]{2,1,0:T(8,128)(2,1)} %y_ref.1, bf16[32,1024]{1,0:T(8,128)(2,1)S(1)} %copy-done.1), custom_call_target="tpu_custom_call" | custom-call | tf_op jit(solution)/shard_map/grams/pallas_call | solution.py:55
  10.3 0.0 copy-start.2
  10.3 1.7 %collective-permute-start = (bf16[33,64,128]{2,1,0:T(8,128)(2,1)S(1)}, bf16[33,64,128]{2,1,0:T(8,128)(2,1)S(1)}, u32[]{:S(2)}, u32[]{:S(2)}) collective-permute-start(bf16[33,64,128]{2,1,0:T(8,128)(2,1)S(1)} %grams.1), channel_id=1, source_target_pairs={{0,1},{1,0},{2,3},{3,2},{4,5},{5,4},{6,7},{7,6},{8,9},{9,8},{10,11... | collective-permute-start | bytes 1622024 | tf_op jit(solution)/shard_map/ppermute | solution.py:275
  11.9 12.3 %collective-permute-done = bf16[33,64,128]{2,1,0:T(8,128)(2,1)S(1)} collective-permute-done((bf16[33,64,128]{2,1,0:T(8,128)(2,1)S(1)}, bf16[33,64,128]{2,1,0:T(8,128)(2,1)S(1)}, u32[]{:S(2)}, u32[]{:S(2)}) %collective-permute-start) | collective-permute-done | bytes 540704 | tf_op jit(solution)/shard_map/ppermute | solution.py:275
  24.2 0.2 add_convert_fusion.own_ref
  24.4 7.6 %collective-permute-start.2 = (bf16[33,64,128]{2,1,0:T(8,128)(2,1)S(1)}, bf16[33,64,128]{2,1,0:T(8,128)(2,1)S(1)}, u32[]{:S(2)}, u32[]{:S(2)}) collective-permute-start(bf16[33,64,128]{2,1,0:T(8,128)(2,1)S(1)} %add_convert_fusion.own_ref), channel_id=1, source_target_pairs={{0,127},{1,126},{2,5},{3,4},{4,3},{5,2},{6,9},{7,8},{8,7},{9,6},{1... | collective-permute-start | bytes 1622024 | tf_op jit(solution)/shard_map/ppermute | solution.py:275
  32.0 0.0 collective-permute-start.1
  32.0 0.0 copy-done.3
  32.0 0.1 copy.11.taperv_ref
  32.1 0.1 reshape.7.taper_ref
  32.2 0.0 copy-done.4
  32.2 0.1 copy.10
  32.3 0.1 reshape.6.idx_ref
  32.4 10.6 %collective-permute-done.2.far_ref = bf16[33,64,128]{2,1,0:T(8,128)(2,1)S(1)} collective-permute-done((bf16[33,64,128]{2,1,0:T(8,128)(2,1)S(1)}, bf16[33,64,128]{2,1,0:T(8,128)(2,1)S(1)}, u32[]{:S(2)}, u32[]{:S(2)}) %collective-permute-start.2) | collective-permute-done | bytes 540704 | tf_op jit(solution)/shard_map/ppermute | solution.py:275
  43.0 0.0 collective-permute-done.1.near_ref
  43.0 57.7 %solve.1.turned_ref = bf16[32,128,128]{2,1,0:T(8,128)(2,1)S(1)} custom-call(s32[160]{0:T(256)S(1)} %reshape.6.idx_ref, f32[160]{0:T(256)S(1)} %reshape.7.taper_ref, s32[32,5]{1,0:T(8,128)S(1)} %fusion.2.idxv_ref, f32[32,5]{1,0:T(8,128)S(1)} %copy.11.taperv_ref, bf16[33,64,128]{2,1,0:T(8,128)(2,1)S(1)} %add_convert_fusion.own_ref, ...), custom_call_target="tpu_custom_call" | custom-call | tf_op jit(solution)/shard_map/solve/pallas_call | solution.py:206
  100.7 0.0 copy-done.2
  100.7 0.0 copy-start
  100.7 2.2 %copy-done = bf16[32,512,128]{2,1,0:T(8,128)(2,1)S(1)} copy-done((bf16[32,512,128]{2,1,0:T(8,128)(2,1)S(1)}, bf16[32,512,128]{2,1,0:T(8,128)(2,1)}, u32[]{:S(2)}) %copy-start) | copy-done | bytes 4194328
  102.9 5.5 %apply.1 = bf16[32,512,128]{2,1,0:T(8,128)(2,1)} custom-call(f32[32,512]{1,0:T(8,128)S(1)} %copy-done.2, bf16[32,128,128]{2,1,0:T(8,128)(2,1)S(1)} %solve.1.turned_ref, bf16[32,512,128]{2,1,0:T(8,128)(2,1)S(1)} %copy-done), custom_call_target="tpu_custom_call" | custom-call | tf_op jit(solution)/shard_map/apply/pallas_call | solution.py:250
  (1 shorter events, 0.0 us)
Async XLA Ops:
  0.7 0.8 copy-start.1
  1.5 30.5 %copy-start.3 = (f32[32,5]{0,1:T(8,128)S(1)}, f32[32,5]{0,1:T(8,128)}, u32[]{:S(2)}) copy-start(f32[32,5]{0,1:T(8,128)} %param.11) | copy-start | bytes 1924
  1.5 30.7 %copy-start.4 = (s32[32,5]{0,1:T(8,128)S(1)}, s32[32,5]{0,1:T(8,128)}, u32[]{:S(2)}) copy-start(s32[32,5]{0,1:T(8,128)} %param.10) | copy-start | bytes 1924
  10.3 90.5 %copy-start.2 = (f32[32,512]{1,0:T(8,128)S(1)}, f32[32,512]{1,0:T(8,128)}, u32[]{:S(2)}) copy-start(f32[32,512]{1,0:T(8,128)} %mean_ref.1) | copy-start | bytes 196612
  10.3 13.9 %collective-permute-start = (bf16[33,64,128]{2,1,0:T(8,128)(2,1)S(1)}, bf16[33,64,128]{2,1,0:T(8,128)(2,1)S(1)}, u32[]{:S(2)}, u32[]{:S(2)}) collective-permute-start(bf16[33,64,128]{2,1,0:T(8,128)(2,1)S(1)} %grams.1), channel_id=1, source_target_pairs={{0,1},{1,0},{2,3},{3,2},{4,5},{5,4},{6,7},{7,6},{8,9},{9,8},{10,11... | collective-permute-start | bytes 1622024 | tf_op jit(solution)/shard_map/ppermute | solution.py:275
  24.4 18.6 %collective-permute-start.2 = (bf16[33,64,128]{2,1,0:T(8,128)(2,1)S(1)}, bf16[33,64,128]{2,1,0:T(8,128)(2,1)S(1)}, u32[]{:S(2)}, u32[]{:S(2)}) collective-permute-start(bf16[33,64,128]{2,1,0:T(8,128)(2,1)S(1)} %add_convert_fusion.own_ref), channel_id=1, source_target_pairs={{0,127},{1,126},{2,5},{3,4},{4,3},{5,2},{6,9},{7,8},{8,7},{9,6},{1... | collective-permute-start | bytes 1622024 | tf_op jit(solution)/shard_map/ppermute | solution.py:275
  32.0 11.0 %collective-permute-start.1 = (bf16[33,64,128]{2,1,0:T(8,128)(2,1)S(1)}, bf16[33,64,128]{2,1,0:T(8,128)(2,1)S(1)}, u32[]{:S(2)}, u32[]{:S(2)}) collective-permute-start(bf16[33,64,128]{2,1,0:T(8,128)(2,1)S(1)} %add_convert_fusion.own_ref), channel_id=1, source_target_pairs={{0,2},{1,3},{2,0},{3,1},{4,6},{5,7},{6,4},{7,5},{8,10},{9,11},{10,... | collective-permute-start | bytes 1622024 | tf_op jit(solution)/shard_map/ppermute | solution.py:275
  100.7 2.2 %copy-start = (bf16[32,512,128]{2,1,0:T(8,128)(2,1)S(1)}, bf16[32,512,128]{2,1,0:T(8,128)(2,1)}, u32[]{:S(2)}) copy-start(bf16[32,512,128]{2,1,0:T(8,128)(2,1)} %param_ref.1) | copy-start | bytes 12582916

commit v2 on v1

v2 whole, which is shorter than its diff:
```python
import functools

import jax
import jax.numpy as jnp
from jax import lax
from jax.experimental import pallas as pl
from jax.experimental.pallas import tpu as pltpu
from jax.sharding import PartitionSpec as P

N = 128
HALF = 64
CHUNK = 16
BLK = 16
U1, U2, U3 = 32, 16, 4
F32 = jnp.float32
BF16 = jnp.bfloat16


def iota(shape, dim):
    return lax.broadcasted_iota(jnp.int32, shape, dim)


def pack(gram):
    top, bottom = gram[:HALF], pltpu.roll(gram[HALF:], HALF, 1)
    return jnp.where(iota((HALF, N), 1) >= iota((HALF, N), 0), top, bottom)


def gram_kernel(step, first, count_ref, y_ref, d_ref, out_ref, diag_ref, proj_ref):
    slots = y_ref.shape[1]
    total = diag_ref.shape[0]
    base = pl.program_id(0) * step
    rows = lax.broadcasted_iota(jnp.int16, (slots, N), 0)
    on_ridge = iota((HALF, N), 0) + HALF == iota((HALF, N), 1)
    start = pl.multiple_of((base // BLK) * BLK, BLK)
    drows = iota((BLK, N), 0)
    d = d_ref[pl.ds(pl.multiple_of(first + start, BLK), BLK), :]
    for s in range(step):
        r = base + s
        live = jnp.clip(count_ref[first + r], 0, slots).astype(jnp.int16)
        y = jnp.where(rows < live, y_ref[s], jnp.zeros((), BF16))
        full = jnp.dot(jnp.concatenate([y.T, d], axis=0), y, preferred_element_type=F32)
        packed = pack(full[:N]).astype(BF16)
        out_ref[2 * r] = packed[:HALF // 2]
        out_ref[2 * r + 1] = packed[HALF // 2:]
        diag_ref[pl.ds(r, 1), :] = jnp.sum(jnp.where(on_ridge, full[HALF:N], 0.0), axis=0, keepdims=True)
        proj_ref[pl.ds(r, 1), :] = jnp.sum(jnp.where(drows == r - start, full[N:], 0.0), axis=0, keepdims=True)

    @pl.when(pl.program_id(0) == pl.num_programs(0) - 1)
    def _():
        out_ref[2 * total] = jnp.concatenate([diag_ref[...], proj_ref[...]], axis=0).astype(BF16)


def grams(live, obs_anomaly, innovation, first, step=8):
    regions, slots, _ = obs_anomaly.shape
    return pl.pallas_call(
        functools.partial(gram_kernel, step, first),
        out_shape=jax.ShapeDtypeStruct((2 * CHUNK + 1, HALF // 2, N), BF16),
        grid_spec=pltpu.PrefetchScalarGridSpec(
            num_scalar_prefetch=1,
            grid=(CHUNK // step,),
            in_specs=[
                pl.BlockSpec((step, slots, N), lambda i, c: (i + first // step, 0, 0)),
                pl.BlockSpec((regions, slots), lambda i, c: (0, 0)),
            ],
            out_specs=pl.BlockSpec((2 * CHUNK + 1, HALF // 2, N), lambda i, c: (0, 0, 0)),
            scratch_shapes=[pltpu.VMEM((CHUNK, N), F32), pltpu.VMEM((CHUNK, N), F32)],
        ),
        compiler_params=pltpu.CompilerParams(vmem_limit_bytes=48 << 20),
        name="grams",
    )(live, obs_anomaly, innovation)


def split(x):
    high = x.astype(BF16)
    return high, (x - high.astype(F32)).astype(BF16)


def expand(pair_packed, diags, mat_ref, row_a, row_b):
    la, lb = pair_packed
    i, j = iota((HALF, N), 0), iota((HALF, N), 1)
    turned = jnp.concatenate([la, lb], axis=0).T
    top, bottom = turned[:HALF], turned[HALF:]
    top_r, bottom_r = pltpu.roll(top, HALF, 1), pltpu.roll(bottom, HALF, 1)
    ridge = jnp.where(i == j, N - 1.0, 0.0)
    for row, lp, tt, tl, tr, dg in (
        (row_a, la, top, bottom, top_r, diags[0]), (row_b, lb, top_r, bottom_r, top, diags[1]),
    ):
        mat_ref[pl.ds(row, HALF), :] = jnp.where(i <= j, lp, tt) + ridge
        corner = jnp.where(i + HALF > j, pltpu.roll(lp, HALF, 1), tr)
        corner = jnp.where(i + HALF == j, dg + (N - 1.0), corner)
        mat_ref[pl.ds(row + HALF, HALF), :] = jnp.where(j < HALF, tl, corner)


def factor(mat_ref, small_ref, regions, kb):
    sub = iota((BLK, regions), 0)
    x = []
    for i in range(BLK):
        row = mat_ref[pl.ds(kb + i, regions, stride=N), :]
        x.append(row.T[kb:kb + BLK])
    lower = []
    for i in range(BLK):
        scale = lax.rsqrt(x[i][i:i + 1])
        r = jnp.where(sub == i, 1.0, x[i]) * scale
        for j in range(i + 1, BLK):
            x[j] = jnp.where(sub == i, 0.0, x[j]) - (x[i][j:j + 1] * scale) * r
        lower.append(jnp.where(sub <= i, r, 0.0))
    inverse = []
    for a in range(BLK):
        z = lower[a][a:a + 1] * lower[a]
        for i in range(a + 1, BLK):
            z = z + lower[i][a:a + 1] * lower[i]
        inverse.append(z)
    per = N // BLK
    lane = iota((regions, N), 1)
    for start, block in ((0, lower), (BLK, inverse)):
        for part in range(BLK // per):
            turned = jnp.concatenate(block[part * per:(part + 1) * per], axis=0).T
            for q in range(per):
                row = jnp.where((lane >= q * BLK) & (lane < (q + 1) * BLK), turned, 0.0)
                small_ref[pl.ds(start + part * per + q, regions, stride=2 * BLK), :] = row


def reduce_rows(mat_ref, small_ref, z_ref, m, kb):
    start = pl.multiple_of(m * N + kb, BLK)
    rows = mat_ref[pl.ds(start, BLK), :]
    lane, sub = iota((BLK, N), 1), iota((BLK, N), 0)
    inside = (lane >= kb) & (lane < kb + BLK)
    rows = jnp.where(inside, jnp.where(lane - kb == sub, 1.0, 0.0), rows)
    rh, rl = split(rows)
    sh, sl = split(small_ref[pl.ds(pl.multiple_of(m * 2 * BLK, 2 * BLK), 2 * BLK), :])
    both = mul3(sh, sl, jnp.concatenate([rh] * (N // BLK), axis=0), jnp.concatenate([rl] * (N // BLK), axis=0))
    mat_ref[pl.ds(start, BLK), :] = jnp.where(lane < kb + BLK, both[:BLK], 0.0)
    z_ref[pl.ds(pl.multiple_of(m * BLK, BLK), BLK), :] = both[BLK:]


def mul3(ah, al, bh, bl):
    return jnp.dot(
        jnp.concatenate([ah, al], axis=1), jnp.concatenate([bh, bh], axis=0),
        preferred_element_type=F32,
    ) + jnp.dot(ah, bl, preferred_element_type=F32)


def update(mat_ref, z_ref, m, kb):
    n = N - kb - BLK
    start = pl.multiple_of(m * N + kb + BLK, BLK)
    mat = mat_ref[pl.ds(start, n), :]
    high, low = split(mat)
    zh, zl = split(z_ref[pl.ds(pl.multiple_of(m * BLK, BLK), BLK), :])
    above, below = jnp.zeros((kb, N), BF16), jnp.zeros((n, N), BF16)

    def place(z):
        return jnp.concatenate([p for p in (above, z, below) if p.shape[0]], axis=0)

    change = mul3(high, low, place(zh), place(zl))
    lane = iota((n, N), 1)
    kept = jnp.where((lane >= kb) & (lane < kb + BLK), 0.0, mat)
    mat_ref[pl.ds(start, n), :] = kept - change


def update_kernel(idx_ref, taper_ref, idxv_ref, taperv_ref, pmean_ref, param_ref, *rest):
    chunks = idxv_ref.shape[0] // CHUNK
    parts, rest = rest[:3 * chunks], rest[3 * chunks:]
    (out_ref, wide_ref, mat_ref, small_ref, z_ref, diag_ref, mean_ref, held_ref, made_ref, sems,
     held_sem, made_sems) = rest
    regions, nb = idxv_ref.shape
    ends = 2 * 3 * regions
    copies = []
    for s, src in enumerate(parts):
        copies.append(pltpu.make_async_copy(
            src.at[pl.ds(0, 2 * CHUNK)], wide_ref.at[pl.ds(s * 2 * CHUNK, 2 * CHUNK)], sems.at[2 * s]))
        copies.append(pltpu.make_async_copy(src.at[2 * CHUNK], wide_ref.at[ends + s], sems.at[2 * s + 1]))
    held = pltpu.make_async_copy(param_ref, held_ref, held_sem)
    for c in copies:
        c.start()
    held.start()
    for c in copies:
        c.wait()
    tails = [wide_ref[ends + s].astype(F32) for s in range(3 * chunks)]
    sel_lane = iota((regions, 3 * regions), 1)
    weights = jnp.zeros((regions, 3 * regions), F32)
    for k in range(nb):
        weights = weights + jnp.where(sel_lane == idxv_ref[:, k:k + 1], taperv_ref[:, k:k + 1], 0.0)
    diag_all = jnp.concatenate([t[:CHUNK] for t in tails], axis=0)
    proj_all = jnp.concatenate([t[CHUNK:] for t in tails], axis=0)
    diag_ref[...] = jnp.dot(weights, diag_all, precision=lax.Precision.HIGHEST, preferred_element_type=F32)
    proj = jnp.dot(weights, proj_all, precision=lax.Precision.HIGHEST, preferred_element_type=F32)

    def combine(pair, _):
        packed = []
        for q in range(2):
            r = 2 * pair + q
            acc = None
            for k in range(nb):
                tile = wide_ref[pl.ds(2 * idx_ref[r * nb + k], 2)].reshape(HALF, N)
                term = taper_ref[r * nb + k] * tile.astype(F32)
                acc = term if acc is None else acc + term
            packed.append(acc)
        row = pl.multiple_of(2 * pair * N, N)
        expand(packed, [diag_ref[pl.ds(2 * pair + q, 1), :] for q in range(2)], mat_ref, row, row + N)
        return 0

    lax.fori_loop(0, regions // 2, combine, 0)
    for kb in range(0, N, BLK):
        factor(mat_ref, small_ref, regions, kb)

        def first(t, _, kb=kb):
            for u in range(U1):
                reduce_rows(mat_ref, small_ref, z_ref, t * U1 + u, kb)
            return 0

        def second(t, _, kb=kb):
            for u in range(U2):
                update(mat_ref, z_ref, t * U2 + u, kb)
            return 0

        lax.fori_loop(0, regions // U1, first, 0)
        if kb + BLK < N:
            lax.fori_loop(0, regions // U2, second, 0)

    def weigh(t, mean):
        for u in range(8):
            w = mat_ref[pl.ds(t * 8 + u, regions, stride=N), :]
            mean = mean + jnp.sum(w * proj, axis=1, keepdims=True) * w
        return mean

    mean_ref[...] = lax.fori_loop(0, N // 8, weigh, jnp.zeros((regions, N), F32))

    left_over = pmean_ref[...]
    pieces = []
    for _ in range(3):
        high = left_over.astype(BF16).astype(F32)
        pieces.append(high)
        left_over = left_over - high
    pieces.append(jnp.zeros((N - 3 * regions, left_over.shape[1]), F32))
    columns = jnp.concatenate(pieces, axis=0).T.astype(BF16)
    held.wait()

    def out_copy(m):
        return pltpu.make_async_copy(made_ref.at[m], out_ref.at[m], made_sems.at[m])

    def finish(t, _):
        lane = iota((N, N), 1)
        for u in range(U3):
            m = t * U3 + u
            w = mat_ref[pl.ds(pl.multiple_of(m * N, N), N), :]
            turned = (jnp.sqrt(jnp.float32(N - 1)) * w + mean_ref[pl.ds(m, 1), :]).astype(BF16)
            pick = ((lane == m) | (lane == regions + m) | (lane == 2 * regions + m)).astype(F32).astype(BF16)
            moved = lax.dot_general(
                jnp.concatenate([held_ref[m], columns], axis=1), jnp.concatenate([turned, pick], axis=1),
                (((1,), (1,)), ((), ())), preferred_element_type=F32,
            )
            made_ref[m] = moved.astype(BF16)
        for u in range(U3):
            out_copy(t * U3 + u).start()
        return 0

    lax.fori_loop(0, regions // U3, finish, 0)
    for m in range(regions):
        out_copy(m).wait()


def solve_update(idx, taper, parts, param_mean, param_anomaly):
    regions, nb = idx.shape
    hbm = pl.BlockSpec(memory_space=pl.ANY)
    smem = pl.BlockSpec(memory_space=pltpu.SMEM)
    vmem = pl.BlockSpec(memory_space=pltpu.VMEM)
    return pl.pallas_call(
        update_kernel,
        out_shape=jax.ShapeDtypeStruct(param_anomaly.shape, BF16),
        in_specs=[smem, smem, vmem, vmem, vmem, hbm] + [hbm] * len(parts),
        out_specs=hbm,
        scratch_shapes=[
            pltpu.VMEM((6 * regions + len(parts), HALF // 2, N), BF16),
            pltpu.VMEM((regions * N, N), F32),
            pltpu.VMEM((regions * 2 * BLK, N), F32),
            pltpu.VMEM((regions * BLK, N), F32),
            pltpu.VMEM((regions, N), F32),
            pltpu.VMEM((regions, N), F32),
            pltpu.VMEM(param_anomaly.shape, BF16),
            pltpu.VMEM(param_anomaly.shape, BF16),
            pltpu.SemaphoreType.DMA((2 * len(parts),)),
            pltpu.SemaphoreType.DMA,
            pltpu.SemaphoreType.DMA((regions,)),
        ],
        compiler_params=pltpu.CompilerParams(vmem_limit_bytes=56 << 20),
        name="solve_update",
    )(idx.reshape(-1), taper.reshape(-1), idx, taper, param_mean, param_anomaly, *parts)


def body(obs_anomaly, innovation, obs_count, neighbour, taper, param_anomaly, param_mean):
    regions, slots = obs_anomaly.shape[:2]
    size, half = lax.axis_size("region"), lax.axis_size("obs")
    total = regions * size
    here, part = lax.axis_index("region"), lax.axis_index("obs")
    devices = [(r, o) for r in range(size) for o in range(half)]

    def swap(x, other):
        line = [(r * half + o, (lambda a: (a[0] % size) * half + a[1])(other(r, o))) for r, o in devices]
        return lax.ppermute(x, ("region", "obs"), line)

    own, near, far = [], [], []
    live = obs_count - part * slots
    for first in range(0, regions, CHUNK):
        packed = grams(live, obs_anomaly, innovation, first)
        partner = swap(packed, lambda r, o: (r, 1 - o))
        both = (packed.astype(F32) + partner.astype(F32)).astype(BF16)
        own.append(both)
        far.append(swap(both, lambda r, o: (r + 1 if r % 2 else r - 1, 1 - o)))
        near.append(swap(both, lambda r, o: (r ^ 1, o)))
    place = (neighbour - here * regions + regions) % total
    even = here % 2 == 0
    before, after = jnp.where(even, 2, 1), jnp.where(even, 1, 2)
    slot = jnp.where(place < regions, before, jnp.where(place < 2 * regions, 0, after))
    idx = (slot * regions + place % regions).astype(jnp.int32)
    return solve_update(idx, taper, own + near + far, param_mean, param_anomaly)


def solution(mesh):
    specs = (
        P("region", "obs", None), P("region", "obs"), P("region"), P("region", None),
        P("region", None), P("region", "obs", None), P("region", "obs"),
    )
    return jax.shard_map(body, mesh=mesh, in_specs=specs, out_specs=P("region", "obs", None), check_vma=False)
```

time: 109 us -> 67.4 us (0.62)
  Pallas kernels: 71.9 us -> 38 us
  waiting for transfers between devices: 22.9 us -> 9.21 us
  starting transfers between devices: 9.27 us -> 15 us
    pallas_call x3, Pallas kernels: 71.9 us -> 38 us  [the longest x1 30.1 us: solve_update(): pl.pallas_call(update_kernel, out_shape=jax.ShapeDtypeStruct(param_anomal...]
    ppermute x3 -> x6, waiting for transfers between devices: 22.9 us -> 9.21 us  [swap(): return lax.ppermute(x, ('region', 'obs'), line)]
    ppermute x3 -> x6, starting transfers between devices: 9.27 us -> 15 us  [swap(): return lax.ppermute(x, ('region', 'obs'), line)]
    reshape x2, local copies, waits for them, and re-layouts: 0.21 us -> 1.33 us  [the longest x1 0.68 us: solve_update(): idx.reshape(-1)]
    unnamed x12 -> x24, local copies, waits for them, and re-layouts: 3.21 us -> 2.39 us
  transfers between devices with their start and end apart: 3 -> 6, of which waited for: 2 -> 2; matrix products, arithmetic and copies ran while one was open for 0% -> 3% of each run, Pallas kernels for 0% -> 6%
where the time goes in v2:
time: 67.4 us; the launch traced here: 67.1 us
  Pallas kernels  38 us (56%)
  starting transfers between devices  15 us (22%)
  waiting for transfers between devices  9.21 us (14%)
  local copies, waits for them, and re-layouts  3.72 us (6%)
  other arithmetic  0.83 us (1%)
    pallas_call x1, Pallas kernels, solve_update(): pl.pallas_call(update_kernel, out_shape=jax.ShapeDtypeStruct(param_anomal...  30.1 us
    ppermute x6, starting transfers between devices, swap(): return lax.ppermute(x, ('region', 'obs'), line)  15 us
    ppermute x6, waiting for transfers between devices, swap(): return lax.ppermute(x, ('region', 'obs'), line)  9.21 us
    pallas_call x2, Pallas kernels, grams(): pl.pallas_call(functools.partial(gram_kernel, step, first), out_shape=jax...  7.93 us
    unnamed x24, local copies, waits for them, and re-layouts  2.39 us
  transfers between devices with their start and end apart: 6, of which 2 were waited for; matrix products, arithmetic and copies ran while one was open for 3% of the time, Pallas kernels for 6%

profile of v2, /device:TPU:0, one launch (start us, length us, event | category | flops | bytes accessed | tf_op | source)
XLA Modules:
  0.0 67.1 jit_solution(2703033541289247167)
XLA Ops:
  0.0 0.7 broadcast_subtract_fusion.count_ref
  0.7 0.8 %copy-done = bf16[32,1024]{1,0:T(8,128)(2,1)S(1)} copy-done((bf16[32,1024]{1,0:T(8,128)(2,1)S(1)}, bf16[32,1024]{1,0:T(8,128)(2,1)}, u32[]{:S(2)}) %copy-start) | copy-done | bytes 65560
  1.5 4.0 %grams.2 = bf16[33,32,128]{2,1,0:T(8,128)(2,1)S(1)} custom-call(s32[32]{0:T(128)S(1)} %broadcast_subtract_fusion.count_ref, bf16[32,1024,128]{2,1,0:T(8,128)(2,1)} %y_ref.3, bf16[32,1024]{1,0:T(8,128)(2,1)S(1)} %copy-done), custom_call_target="tpu_custom_call" | custom-call | tf_op jit(solution)/shard_map/grams/pallas_call | solution.py:55
  5.5 0.0 copy-start.9
  5.5 0.0 copy-start.10
  5.5 1.7 %collective-permute-start = (bf16[33,32,128]{2,1,0:T(8,128)(2,1)S(1)}, bf16[33,32,128]{2,1,0:T(8,128)(2,1)S(1)}, u32[]{:S(2)}, u32[]{:S(2)}) collective-permute-start(bf16[33,32,128]{2,1,0:T(8,128)(2,1)S(1)} %grams.2), channel_id=1, source_target_pairs={{0,1},{1,0},{2,3},{3,2},{4,5},{5,4},{6,7},{7,6},{8,9},{9,8},{10,11... | collective-permute-start | bytes 811016 | tf_op jit(solution)/shard_map/ppermute | solution.py:299
  7.1 4.0 %grams.3 = bf16[33,32,128]{2,1,0:T(8,128)(2,1)S(1)} custom-call(s32[32]{0:T(128)S(1)} %broadcast_subtract_fusion.count_ref, bf16[32,1024,128]{2,1,0:T(8,128)(2,1)} %y_ref.3, bf16[32,1024]{1,0:T(8,128)(2,1)S(1)} %copy-done), custom_call_target="tpu_custom_call" | custom-call | tf_op jit(solution)/shard_map/grams/pallas_call | solution.py:55
  11.1 0.5 collective-permute-start.1
  11.7 2.4 %collective-permute-done = bf16[33,32,128]{2,1,0:T(8,128)(2,1)S(1)} collective-permute-done((bf16[33,32,128]{2,1,0:T(8,128)(2,1)S(1)}, bf16[33,32,128]{2,1,0:T(8,128)(2,1)S(1)}, u32[]{:S(2)}, u32[]{:S(2)}) %collective-permute-start) | collective-permute-done | bytes 270368 | tf_op jit(solution)/shard_map/ppermute | solution.py:299
  14.0 0.1 add_convert_fusion.1.rest_0_
  14.1 0.0 copy-start.1
  14.1 7.2 %collective-permute-start.4 = (bf16[33,32,128]{2,1,0:T(8,128)(2,1)S(1)}, bf16[33,32,128]{2,1,0:T(8,128)(2,1)S(1)}, u32[]{:S(2)}, u32[]{:S(2)}) collective-permute-start(bf16[33,32,128]{2,1,0:T(8,128)(2,1)S(1)} %add_convert_fusion.1.rest_0_), channel_id=1, source_target_pairs={{0,127},{1,126},{2,5},{3,4},{4,3},{5,2},{6,9},{7,8},{8,7},{9,6},{1... | collective-permute-start | bytes 811016 | tf_op jit(solution)/shard_map/ppermute | solution.py:299
  21.3 0.0 collective-permute-start.2
  21.3 0.0 collective-permute-done.1
  21.3 0.1 add_convert_fusion.rest_1_
  21.4 0.0 copy-start.2
  21.4 5.7 %collective-permute-start.5 = (bf16[33,32,128]{2,1,0:T(8,128)(2,1)S(1)}, bf16[33,32,128]{2,1,0:T(8,128)(2,1)S(1)}, u32[]{:S(2)}, u32[]{:S(2)}) collective-permute-start(bf16[33,32,128]{2,1,0:T(8,128)(2,1)S(1)} %add_convert_fusion.rest_1_), channel_id=1, source_target_pairs={{0,127},{1,126},{2,5},{3,4},{4,3},{5,2},{6,9},{7,8},{8,7},{9,6},{1... | collective-permute-start | bytes 811016 | tf_op jit(solution)/shard_map/ppermute | solution.py:299
  27.1 0.0 collective-permute-start.3
  27.1 0.0 copy-done.9
  27.1 0.1 copy.11.taperv_ref
  27.2 0.7 reshape.7.taper_ref
  27.8 0.1 copy.10
  28.0 0.7 %reshape.6.idx_ref = s32[160]{0:T(256)} reshape(s32[32,5]{1,0:T(8,128)S(1)} %fusion.2.idxv_ref) | data formatting | bytes 1280 | tf_op jit(solution)/shard_map/reshape | solution.py:287
  28.6 0.0 collective-permute-done.4.rest_4_
  28.6 0.0 collective-permute-done.2.rest_2_
  28.6 0.0 copy-start.4
  28.7 6.8 %collective-permute-done.5.rest_5_ = bf16[33,32,128]{2,1,0:T(8,128)(2,1)S(1)} collective-permute-done((bf16[33,32,128]{2,1,0:T(8,128)(2,1)S(1)}, bf16[33,32,128]{2,1,0:T(8,128)(2,1)S(1)}, u32[]{:S(2)}, u32[]{:S(2)}) %collective-permute-start.5) | collective-permute-done | bytes 270368 | tf_op jit(solution)/shard_map/ppermute | solution.py:299
  35.5 0.0 collective-permute-done.3.rest_3_
  35.5 0.0 copy-done.1
  35.5 0.6 copy-done.5
  36.2 0.7 %copy-done.6 = bf16[33,32,128]{2,1,0:T(8,128)(2,1)} copy-done((bf16[33,32,128]{2,1,0:T(8,128)(2,1)}, bf16[33,32,128]{2,1,0:T(8,128)(2,1)S(1)}, u32[]{:S(2)}) %copy-start.6) | copy-done | bytes 270360
  36.9 30.1 %solve_update.1 = bf16[32,512,128]{2,1,0:T(8,128)(2,1)} custom-call(s32[160]{0:T(256)} %reshape.6.idx_ref, f32[160]{0:T(256)} %reshape.7.taper_ref, s32[32,5]{1,0:T(8,128)} %copy-done.8, f32[32,5]{1,0:T(8,128)} %copy-done.7, f32[32,512]{1,0:T(8,128)} %pmean_ref.1, bf16[32,512,128]{2,1,0:T(8,128)(2,1)} %param_ref.1, bf16[33,32,128]{2,1,0:T(8,128)(2,1)} %copy-done.1, ...), custom_call_target="tpu_custom_call" | custom-call | tf_op jit(solution)/shard_map/solve_update/pallas_call | solution.py:267
  (13 shorter events, 0.1 us)
Async XLA Ops:
  0.7 0.8 %copy-start = (bf16[32,1024]{1,0:T(8,128)(2,1)S(1)}, bf16[32,1024]{1,0:T(8,128)(2,1)}, u32[]{:S(2)}) copy-start(bf16[32,1024]{1,0:T(8,128)(2,1)} %d_ref.3) | copy-start | bytes 196612
  5.5 21.6 %copy-start.9 = (f32[32,5]{0,1:T(8,128)S(1)}, f32[32,5]{0,1:T(8,128)}, u32[]{:S(2)}) copy-start(f32[32,5]{0,1:T(8,128)} %param.11) | copy-start | bytes 1924
  5.5 22.3 %copy-start.10 = (s32[32,5]{0,1:T(8,128)S(1)}, s32[32,5]{0,1:T(8,128)}, u32[]{:S(2)}) copy-start(s32[32,5]{0,1:T(8,128)} %param.10) | copy-start | bytes 1924
  5.5 8.5 %collective-permute-start = (bf16[33,32,128]{2,1,0:T(8,128)(2,1)S(1)}, bf16[33,32,128]{2,1,0:T(8,128)(2,1)S(1)}, u32[]{:S(2)}, u32[]{:S(2)}) collective-permute-start(bf16[33,32,128]{2,1,0:T(8,128)(2,1)S(1)} %grams.2), channel_id=1, source_target_pairs={{0,1},{1,0},{2,3},{3,2},{4,5},{5,4},{6,7},{7,6},{8,9},{9,8},{10,11... | collective-permute-start | bytes 811016 | tf_op jit(solution)/shard_map/ppermute | solution.py:299
  11.1 10.2 %collective-permute-start.1 = (bf16[33,32,128]{2,1,0:T(8,128)(2,1)S(1)}, bf16[33,32,128]{2,1,0:T(8,128)(2,1)S(1)}, u32[]{:S(2)}, u32[]{:S(2)}) collective-permute-start(bf16[33,32,128]{2,1,0:T(8,128)(2,1)S(1)} %grams.3), channel_id=1, source_target_pairs={{0,1},{1,0},{2,3},{3,2},{4,5},{5,4},{6,7},{7,6},{8,9},{9,8},{10,11... | collective-permute-start | bytes 811016 | tf_op jit(solution)/shard_map/ppermute | solution.py:299
  14.1 21.4 %copy-start.1 = (bf16[33,32,128]{2,1,0:T(8,128)(2,1)}, bf16[33,32,128]{2,1,0:T(8,128)(2,1)S(1)}, u32[]{:S(2)}) copy-start(bf16[33,32,128]{2,1,0:T(8,128)(2,1)S(1)} %add_convert_fusion.1.rest_0_) | copy-start | bytes 811012
  14.1 14.5 %collective-permute-start.4 = (bf16[33,32,128]{2,1,0:T(8,128)(2,1)S(1)}, bf16[33,32,128]{2,1,0:T(8,128)(2,1)S(1)}, u32[]{:S(2)}, u32[]{:S(2)}) collective-permute-start(bf16[33,32,128]{2,1,0:T(8,128)(2,1)S(1)} %add_convert_fusion.1.rest_0_), channel_id=1, source_target_pairs={{0,127},{1,126},{2,5},{3,4},{4,3},{5,2},{6,9},{7,8},{8,7},{9,6},{1... | collective-permute-start | bytes 811016 | tf_op jit(solution)/shard_map/ppermute | solution.py:299
  21.3 7.4 %collective-permute-start.2 = (bf16[33,32,128]{2,1,0:T(8,128)(2,1)S(1)}, bf16[33,32,128]{2,1,0:T(8,128)(2,1)S(1)}, u32[]{:S(2)}, u32[]{:S(2)}) collective-permute-start(bf16[33,32,128]{2,1,0:T(8,128)(2,1)S(1)} %add_convert_fusion.1.rest_0_), channel_id=1, source_target_pairs={{0,2},{1,3},{2,0},{3,1},{4,6},{5,7},{6,4},{7,5},{8,10},{9,11},{10,... | collective-permute-start | bytes 811016 | tf_op jit(solution)/shard_map/ppermute | solution.py:299
  21.4 14.1 %copy-start.2 = (bf16[33,32,128]{2,1,0:T(8,128)(2,1)}, bf16[33,32,128]{2,1,0:T(8,128)(2,1)S(1)}, u32[]{:S(2)}) copy-start(bf16[33,32,128]{2,1,0:T(8,128)(2,1)S(1)} %add_convert_fusion.rest_1_) | copy-start | bytes 811012
  21.4 14.1 %collective-permute-start.5 = (bf16[33,32,128]{2,1,0:T(8,128)(2,1)S(1)}, bf16[33,32,128]{2,1,0:T(8,128)(2,1)S(1)}, u32[]{:S(2)}, u32[]{:S(2)}) collective-permute-start(bf16[33,32,128]{2,1,0:T(8,128)(2,1)S(1)} %add_convert_fusion.rest_1_), channel_id=1, source_target_pairs={{0,127},{1,126},{2,5},{3,4},{4,3},{5,2},{6,9},{7,8},{8,7},{9,6},{1... | collective-permute-start | bytes 811016 | tf_op jit(solution)/shard_map/ppermute | solution.py:299
  27.1 8.4 %collective-permute-start.3 = (bf16[33,32,128]{2,1,0:T(8,128)(2,1)S(1)}, bf16[33,32,128]{2,1,0:T(8,128)(2,1)S(1)}, u32[]{:S(2)}, u32[]{:S(2)}) collective-permute-start(bf16[33,32,128]{2,1,0:T(8,128)(2,1)S(1)} %add_convert_fusion.rest_1_), channel_id=1, source_target_pairs={{0,2},{1,3},{2,0},{3,1},{4,6},{5,7},{6,4},{7,5},{8,10},{9,11},{10,... | collective-permute-start | bytes 811016 | tf_op jit(solution)/shard_map/ppermute | solution.py:299
  27.2 8.3 %copy-start.7 = (f32[32,5]{1,0:T(8,128)}, f32[32,5]{1,0:T(8,128)S(1)}, u32[]{:S(2)}) copy-start(f32[32,5]{1,0:T(8,128)S(1)} %copy.11.taperv_ref) | copy-start | bytes 1924
  27.9 7.6 %copy-start.8 = (s32[32,5]{1,0:T(8,128)}, s32[32,5]{1,0:T(8,128)S(1)}, u32[]{:S(2)}) copy-start(s32[32,5]{1,0:T(8,128)S(1)} %fusion.2.idxv_ref) | copy-start | bytes 1924
  28.6 6.9 %copy-start.3 = (bf16[33,32,128]{2,1,0:T(8,128)(2,1)}, bf16[33,32,128]{2,1,0:T(8,128)(2,1)S(1)}, u32[]{:S(2)}) copy-start(bf16[33,32,128]{2,1,0:T(8,128)(2,1)S(1)} %collective-permute-done.4.rest_4_) | copy-start | bytes 811012
  28.6 6.9 %copy-start.4 = (bf16[33,32,128]{2,1,0:T(8,128)(2,1)}, bf16[33,32,128]{2,1,0:T(8,128)(2,1)S(1)}, u32[]{:S(2)}) copy-start(bf16[33,32,128]{2,1,0:T(8,128)(2,1)S(1)} %collective-permute-done.2.rest_2_) | copy-start | bytes 811012
  35.5 0.7 %copy-start.5 = (bf16[33,32,128]{2,1,0:T(8,128)(2,1)}, bf16[33,32,128]{2,1,0:T(8,128)(2,1)S(1)}, u32[]{:S(2)}) copy-start(bf16[33,32,128]{2,1,0:T(8,128)(2,1)S(1)} %collective-permute-done.5.rest_5_) | copy-start | bytes 811012
  36.2 0.7 %copy-start.6 = (bf16[33,32,128]{2,1,0:T(8,128)(2,1)}, bf16[33,32,128]{2,1,0:T(8,128)(2,1)S(1)}, u32[]{:S(2)}) copy-start(bf16[33,32,128]{2,1,0:T(8,128)(2,1)S(1)} %collective-permute-done.3.rest_3_) | copy-start | bytes 811012

commit v3 on v2

--- a/solution.py
+++ b/solution.py
@@ -11,7 +11,7 @@
 HALF = 64
 CHUNK = 16
 BLK = 16
-U1, U2, U3 = 32, 16, 4
+U1, U2, U3 = 32, 32, 8
 F32 = jnp.float32
 BF16 = jnp.bfloat16
 
@@ -31,12 +31,12 @@
     base = pl.program_id(0) * step
     rows = lax.broadcasted_iota(jnp.int16, (slots, N), 0)
     on_ridge = iota((HALF, N), 0) + HALF == iota((HALF, N), 1)
-    start = pl.multiple_of((base // BLK) * BLK, BLK)
-    drows = iota((BLK, N), 0)
-    d = d_ref[pl.ds(pl.multiple_of(first + start, BLK), BLK), :]
+    start = pl.multiple_of((base // 16) * 16, 16)
+    drows = iota((16, N), 0)
+    d = d_ref[pl.ds(pl.multiple_of(first + start, 16), 16), :]
     for s in range(step):
         r = base + s
-        live = jnp.clip(count_ref[first + r], 0, slots).astype(jnp.int16)
+        live = jnp.clip(count_ref[first + r] - lax.axis_index("obs") * slots, 0, slots).astype(jnp.int16)
         y = jnp.where(rows < live, y_ref[s], jnp.zeros((), BF16))
         full = jnp.dot(jnp.concatenate([y.T, d], axis=0), y, preferred_element_type=F32)
         packed = pack(full[:N]).astype(BF16)
@@ -50,7 +50,7 @@
         out_ref[2 * total] = jnp.concatenate([diag_ref[...], proj_ref[...]], axis=0).astype(BF16)
 
 
-def grams(live, obs_anomaly, innovation, first, step=8):
+def grams(obs_count, obs_anomaly, innovation, first, step=8):
     regions, slots, _ = obs_anomaly.shape
     return pl.pallas_call(
         functools.partial(gram_kernel, step, first),
@@ -67,7 +67,7 @@
         ),
         compiler_params=pltpu.CompilerParams(vmem_limit_bytes=48 << 20),
         name="grams",
-    )(live, obs_anomaly, innovation)
+    )(obs_count, obs_anomaly, innovation)
 
 
 def split(x):
@@ -128,16 +128,22 @@
     rows = jnp.where(inside, jnp.where(lane - kb == sub, 1.0, 0.0), rows)
     rh, rl = split(rows)
     sh, sl = split(small_ref[pl.ds(pl.multiple_of(m * 2 * BLK, 2 * BLK), 2 * BLK), :])
-    both = mul3(sh, sl, jnp.concatenate([rh] * (N // BLK), axis=0), jnp.concatenate([rl] * (N // BLK), axis=0))
+    both = mul_m(sh, sl, jnp.concatenate([rh] * (N // BLK), axis=0), jnp.concatenate([rl] * (N // BLK), axis=0))
     mat_ref[pl.ds(start, BLK), :] = jnp.where(lane < kb + BLK, both[:BLK], 0.0)
     z_ref[pl.ds(pl.multiple_of(m * BLK, BLK), BLK), :] = both[BLK:]
 
 
-def mul3(ah, al, bh, bl):
-    return jnp.dot(
-        jnp.concatenate([ah, al], axis=1), jnp.concatenate([bh, bh], axis=0),
-        preferred_element_type=F32,
-    ) + jnp.dot(ah, bl, preferred_element_type=F32)
+def mul_k(ah, al, bh, bl):
+    right = jnp.concatenate([
+        jnp.concatenate([bh, bl], axis=1), jnp.concatenate([bh, jnp.zeros_like(bl)], axis=1)], axis=0)
+    both = jnp.dot(jnp.concatenate([ah, al], axis=1), right, preferred_element_type=F32)
+    return both[:, :N] + both[:, N:]
+
+
+def mul_m(ah, al, bh, bl):
+    n = ah.shape[0]
+    both = jnp.dot(jnp.concatenate([ah, al], axis=0), jnp.concatenate([bh, bl], axis=1), preferred_element_type=F32)
+    return (both[:n, :N] + both[:n, N:]) + both[n:, :N]
 
 
 def update(mat_ref, z_ref, m, kb):
@@ -151,7 +157,7 @@
     def place(z):
         return jnp.concatenate([p for p in (above, z, below) if p.shape[0]], axis=0)
 
-    change = mul3(high, low, place(zh), place(zl))
+    change = mul_k(high, low, place(zh), place(zl))
     lane = iota((n, N), 1)
     kept = jnp.where((lane >= kb) & (lane < kb + BLK), 0.0, mat)
     mat_ref[pl.ds(start, n), :] = kept - change
@@ -191,15 +197,15 @@
             r = 2 * pair + q
             acc = None
             for k in range(nb):
-                tile = wide_ref[pl.ds(2 * idx_ref[r * nb + k], 2)].reshape(HALF, N)
-                term = taper_ref[r * nb + k] * tile.astype(F32)
+                tile = wide_ref[pl.ds(2 * idx_ref[r, k], 2)].reshape(HALF, N)
+                term = taper_ref[r, k] * tile.astype(F32)
                 acc = term if acc is None else acc + term
             packed.append(acc)
         row = pl.multiple_of(2 * pair * N, N)
         expand(packed, [diag_ref[pl.ds(2 * pair + q, 1), :] for q in range(2)], mat_ref, row, row + N)
         return 0
 
-    lax.fori_loop(0, regions // 2, combine, 0)
+    lax.fori_loop(0, regions // 2, combine, 0, unroll=8)
     for kb in range(0, N, BLK):
         factor(mat_ref, small_ref, regions, kb)
 
@@ -218,12 +224,12 @@
             lax.fori_loop(0, regions // U2, second, 0)
 
     def weigh(t, mean):
-        for u in range(8):
-            w = mat_ref[pl.ds(t * 8 + u, regions, stride=N), :]
+        for u in range(32):
+            w = mat_ref[pl.ds(t * 32 + u, regions, stride=N), :]
             mean = mean + jnp.sum(w * proj, axis=1, keepdims=True) * w
         return mean
 
-    mean_ref[...] = lax.fori_loop(0, N // 8, weigh, jnp.zeros((regions, N), F32))
+    mean_ref[...] = lax.fori_loop(0, N // 32, weigh, jnp.zeros((regions, N), F32))
 
     left_over = pmean_ref[...]
     pieces = []
@@ -284,14 +290,14 @@
         ],
         compiler_params=pltpu.CompilerParams(vmem_limit_bytes=56 << 20),
         name="solve_update",
-    )(idx.reshape(-1), taper.reshape(-1), idx, taper, param_mean, param_anomaly, *parts)
+    )(idx, taper, idx, taper, param_mean, param_anomaly, *parts)
 
 
 def body(obs_anomaly, innovation, obs_count, neighbour, taper, param_anomaly, param_mean):
-    regions, slots = obs_anomaly.shape[:2]
+    regions = obs_anomaly.shape[0]
     size, half = lax.axis_size("region"), lax.axis_size("obs")
     total = regions * size
-    here, part = lax.axis_index("region"), lax.axis_index("obs")
+    here = lax.axis_index("region")
     devices = [(r, o) for r in range(size) for o in range(half)]
 
     def swap(x, other):
@@ -299,9 +305,8 @@
         return lax.ppermute(x, ("region", "obs"), line)
 
     own, near, far = [], [], []
-    live = obs_count - part * slots
     for first in range(0, regions, CHUNK):
-        packed = grams(live, obs_anomaly, innovation, first)
+        packed = grams(obs_count, obs_anomaly, innovation, first)
         partner = swap(packed, lambda r, o: (r, 1 - o))
         both = (packed.astype(F32) + partner.astype(F32)).astype(BF16)
         own.append(both)

time: 67.4 us -> 59.9 us (0.89)
  Pallas kernels: 38 us -> 30.6 us
    pallas_call x1, Pallas kernels: 30.1 us -> 22.6 us  [solve_update(): pl.pallas_call(update_kernel, out_shape=jax.ShapeDtypeStruct(param_anomal...]
    reshape x2 -> x0, local copies, waits for them, and re-layouts: 1.33 us -> none  [the longest x1 0.68 us: solve_update(): idx.reshape(-1)]
    unnamed x24 -> x22, local copies, waits for them, and re-layouts: 2.39 us -> 3.67 us
  transfers between devices with their start and end apart: 6 -> 6, of which waited for: 2 -> 2; matrix products, arithmetic and copies ran while one was open for 3% -> 3% of each run, Pallas kernels for 6% -> 7%
where the time goes in v3:
time: 59.9 us; the launch traced here: 59.7 us
  Pallas kernels  30.6 us (51%)
  starting transfers between devices  15.1 us (25%)
  waiting for transfers between devices  9.34 us (16%)
  local copies, waits for them, and re-layouts  3.67 us (6%)
  other arithmetic  0.77 us (1%)
    pallas_call x1, Pallas kernels, solve_update(): pl.pallas_call(update_kernel, out_shape=jax.ShapeDtypeStruct(param_anomal...  22.6 us
    ppermute x6, starting transfers between devices, swap(): return lax.ppermute(x, ('region', 'obs'), line)  15.1 us
    ppermute x6, waiting for transfers between devices, swap(): return lax.ppermute(x, ('region', 'obs'), line)  9.34 us
    pallas_call x2, Pallas kernels, grams(): pl.pallas_call(functools.partial(gram_kernel, step, first), out_shape=jax...  7.96 us
    unnamed x22, local copies, waits for them, and re-layouts  3.67 us
  transfers between devices with their start and end apart: 6, of which 2 were waited for; matrix products, arithmetic and copies ran while one was open for 3% of the time, Pallas kernels for 7%

profile of v3, /device:TPU:0, one launch (start us, length us, event | category | flops | bytes accessed | tf_op | source)
XLA Modules:
  0.0 59.7 jit_solution(16608557151491031439)
XLA Ops:
  0.0 0.8 %copy-done = bf16[32,1024]{1,0:T(8,128)(2,1)S(1)} copy-done((bf16[32,1024]{1,0:T(8,128)(2,1)S(1)}, bf16[32,1024]{1,0:T(8,128)(2,1)}, u32[]{:S(2)}) %copy-start) | copy-done | bytes 65560
  0.8 0.7 %copy-done.1 = s32[32]{0:T(128)S(1)} copy-done((s32[32]{0:T(128)S(1)}, s32[32]{0:T(128)}, u32[]{:S(2)}) %copy-start.1) | copy-done | bytes 152
  1.5 4.0 %grams.2 = bf16[33,32,128]{2,1,0:T(8,128)(2,1)S(1)} custom-call(s32[32]{0:T(128)S(1)} %copy-done.1, bf16[32,1024,128]{2,1,0:T(8,128)(2,1)} %y_ref.3, bf16[32,1024]{1,0:T(8,128)(2,1)S(1)} %copy-done), custom_call_target="tpu_custom_call" | custom-call | tf_op jit(solution)/shard_map/grams/pallas_call | solution.py:55
  5.5 0.0 copy-start.8
  5.5 0.0 copy-start.9
  5.5 1.6 %collective-permute-start = (bf16[33,32,128]{2,1,0:T(8,128)(2,1)S(1)}, bf16[33,32,128]{2,1,0:T(8,128)(2,1)S(1)}, u32[]{:S(2)}, u32[]{:S(2)}) collective-permute-start(bf16[33,32,128]{2,1,0:T(8,128)(2,1)S(1)} %grams.2), channel_id=1, source_target_pairs={{0,1},{1,0},{2,3},{3,2},{4,5},{5,4},{6,7},{7,6},{8,9},{9,8},{10,11... | collective-permute-start | bytes 811016 | tf_op jit(solution)/shard_map/ppermute | solution.py:305
  7.2 4.0 %grams.3 = bf16[33,32,128]{2,1,0:T(8,128)(2,1)S(1)} custom-call(s32[32]{0:T(128)S(1)} %copy-done.1, bf16[32,1024,128]{2,1,0:T(8,128)(2,1)} %y_ref.3, bf16[32,1024]{1,0:T(8,128)(2,1)S(1)} %copy-done), custom_call_target="tpu_custom_call" | custom-call | tf_op jit(solution)/shard_map/grams/pallas_call | solution.py:55
  11.1 0.5 collective-permute-start.1
  11.7 2.4 %collective-permute-done = bf16[33,32,128]{2,1,0:T(8,128)(2,1)S(1)} collective-permute-done((bf16[33,32,128]{2,1,0:T(8,128)(2,1)S(1)}, bf16[33,32,128]{2,1,0:T(8,128)(2,1)S(1)}, u32[]{:S(2)}, u32[]{:S(2)}) %collective-permute-start) | collective-permute-done | bytes 270368 | tf_op jit(solution)/shard_map/ppermute | solution.py:305
  14.0 0.1 add_convert_fusion.1.rest_0_
  14.1 0.0 copy-start.2
  14.1 7.2 %collective-permute-start.4 = (bf16[33,32,128]{2,1,0:T(8,128)(2,1)S(1)}, bf16[33,32,128]{2,1,0:T(8,128)(2,1)S(1)}, u32[]{:S(2)}, u32[]{:S(2)}) collective-permute-start(bf16[33,32,128]{2,1,0:T(8,128)(2,1)S(1)} %add_convert_fusion.1.rest_0_), channel_id=1, source_target_pairs={{0,127},{1,126},{2,5},{3,4},{4,3},{5,2},{6,9},{7,8},{8,7},{9,6},{1... | collective-permute-start | bytes 811016 | tf_op jit(solution)/shard_map/ppermute | solution.py:305
  21.3 0.0 collective-permute-start.2
  21.3 0.0 collective-permute-done.1
  21.3 0.1 add_convert_fusion.rest_1_
  21.4 0.0 copy-start.3
  21.4 5.7 %collective-permute-start.5 = (bf16[33,32,128]{2,1,0:T(8,128)(2,1)S(1)}, bf16[33,32,128]{2,1,0:T(8,128)(2,1)S(1)}, u32[]{:S(2)}, u32[]{:S(2)}) collective-permute-start(bf16[33,32,128]{2,1,0:T(8,128)(2,1)S(1)} %add_convert_fusion.rest_1_), channel_id=1, source_target_pairs={{0,127},{1,126},{2,5},{3,4},{4,3},{5,2},{6,9},{7,8},{8,7},{9,6},{1... | collective-permute-start | bytes 811016 | tf_op jit(solution)/shard_map/ppermute | solution.py:305
  27.1 0.0 collective-permute-start.3
  27.1 0.0 copy-done.8
  27.1 0.1 copy.8
  27.2 0.0 copy-done.9
  27.2 0.7 %copy.9.taper_ref.taperv_ref = f32[32,5]{1,0:T(8,128)} copy(f32[32,5]{0,1:T(8,128)S(1)} %copy-done.9) | data formatting | bytes 1280 | tf_op args[4]
  27.9 0.6 %fusion.2.idx_ref.idxv_ref = s32[32,5]{1,0:T(8,128)} fusion(s32[32,5]{1,0:T(8,128)S(1)} %copy.8, s32[]{:T(128)S(6)} %select_n.35, s32[]{:T(128)S(6)} %select_n.34, s32[]{:T(128)S(6)} %mul.6), kind=kLoop, calls=%fused_computation.10 | loop fusion | flops 4800 | bytes 1292 | tf_op jit(solution)/shard_map/add | solution.py:319
  28.5 0.0 collective-permute-done.4.rest_4_
  28.5 0.0 collective-permute-done.2.rest_2_
  28.5 0.0 copy-start.5
  28.5 7.0 %collective-permute-done.5.rest_5_ = bf16[33,32,128]{2,1,0:T(8,128)(2,1)S(1)} collective-permute-done((bf16[33,32,128]{2,1,0:T(8,128)(2,1)S(1)}, bf16[33,32,128]{2,1,0:T(8,128)(2,1)S(1)}, u32[]{:S(2)}, u32[]{:S(2)}) %collective-permute-start.5) | collective-permute-done | bytes 270368 | tf_op jit(solution)/shard_map/ppermute | solution.py:305
  35.5 0.0 collective-permute-done.3.rest_3_
  35.5 0.0 copy-done.2
  35.5 0.7 %copy-done.6 = bf16[33,32,128]{2,1,0:T(8,128)(2,1)} copy-done((bf16[33,32,128]{2,1,0:T(8,128)(2,1)}, bf16[33,32,128]{2,1,0:T(8,128)(2,1)S(1)}, u32[]{:S(2)}) %copy-start.6) | copy-done | bytes 270360
  36.2 0.7 %copy-done.7 = bf16[33,32,128]{2,1,0:T(8,128)(2,1)} copy-done((bf16[33,32,128]{2,1,0:T(8,128)(2,1)}, bf16[33,32,128]{2,1,0:T(8,128)(2,1)S(1)}, u32[]{:S(2)}) %copy-start.7) | copy-done | bytes 270360
  36.9 22.6 %solve_update.1 = bf16[32,512,128]{2,1,0:T(8,128)(2,1)} custom-call(s32[32,5]{1,0:T(8,128)} %fusion.2.idx_ref.idxv_ref, f32[32,5]{1,0:T(8,128)} %copy.9.taper_ref.taperv_ref, s32[32,5]{1,0:T(8,128)} %fusion.2.idx_ref.idxv_ref, f32[32,5]{1,0:T(8,128)} %copy.9.taper_ref.taperv_ref, f32[32,512]{1,0:T(8,128)} %pmean_ref.1, bf16[32,512,128]{2,1,0:T(8,128)(2,1)} %param_ref.1, ...), custom_call_target="tpu_custom_call" | custom-call | tf_op jit(solution)/shard_map/solve_update/pallas_call | solution.py:273
  (8 shorter events, 0.0 us)
Async XLA Ops:
  0.0 0.8 %copy-start = (bf16[32,1024]{1,0:T(8,128)(2,1)S(1)}, bf16[32,1024]{1,0:T(8,128)(2,1)}, u32[]{:S(2)}) copy-start(bf16[32,1024]{1,0:T(8,128)(2,1)} %d_ref.3) | copy-start | bytes 196612
  0.8 0.7 %copy-start.1 = (s32[32]{0:T(128)S(1)}, s32[32]{0:T(128)}, u32[]{:S(2)}) copy-start(s32[32]{0:T(128)} %count_ref.3) | copy-start | bytes 388
  5.5 21.6 %copy-start.8 = (s32[32,5]{0,1:T(8,128)S(1)}, s32[32,5]{0,1:T(8,128)}, u32[]{:S(2)}) copy-start(s32[32,5]{0,1:T(8,128)} %param.10) | copy-start | bytes 1924
  5.5 21.7 %copy-start.9 = (f32[32,5]{0,1:T(8,128)S(1)}, f32[32,5]{0,1:T(8,128)}, u32[]{:S(2)}) copy-start(f32[32,5]{0,1:T(8,128)} %param.11) | copy-start | bytes 1924
  5.5 8.5 %collective-permute-start = (bf16[33,32,128]{2,1,0:T(8,128)(2,1)S(1)}, bf16[33,32,128]{2,1,0:T(8,128)(2,1)S(1)}, u32[]{:S(2)}, u32[]{:S(2)}) collective-permute-start(bf16[33,32,128]{2,1,0:T(8,128)(2,1)S(1)} %grams.2), channel_id=1, source_target_pairs={{0,1},{1,0},{2,3},{3,2},{4,5},{5,4},{6,7},{7,6},{8,9},{9,8},{10,11... | collective-permute-start | bytes 811016 | tf_op jit(solution)/shard_map/ppermute | solution.py:305
  11.1 10.2 %collective-permute-start.1 = (bf16[33,32,128]{2,1,0:T(8,128)(2,1)S(1)}, bf16[33,32,128]{2,1,0:T(8,128)(2,1)S(1)}, u32[]{:S(2)}, u32[]{:S(2)}) collective-permute-start(bf16[33,32,128]{2,1,0:T(8,128)(2,1)S(1)} %grams.3), channel_id=1, source_target_pairs={{0,1},{1,0},{2,3},{3,2},{4,5},{5,4},{6,7},{7,6},{8,9},{9,8},{10,11... | collective-permute-start | bytes 811016 | tf_op jit(solution)/shard_map/ppermute | solution.py:305
  14.1 21.4 %copy-start.2 = (bf16[33,32,128]{2,1,0:T(8,128)(2,1)}, bf16[33,32,128]{2,1,0:T(8,128)(2,1)S(1)}, u32[]{:S(2)}) copy-start(bf16[33,32,128]{2,1,0:T(8,128)(2,1)S(1)} %add_convert_fusion.1.rest_0_) | copy-start | bytes 811012
  14.1 14.4 %collective-permute-start.4 = (bf16[33,32,128]{2,1,0:T(8,128)(2,1)S(1)}, bf16[33,32,128]{2,1,0:T(8,128)(2,1)S(1)}, u32[]{:S(2)}, u32[]{:S(2)}) collective-permute-start(bf16[33,32,128]{2,1,0:T(8,128)(2,1)S(1)} %add_convert_fusion.1.rest_0_), channel_id=1, source_target_pairs={{0,127},{1,126},{2,5},{3,4},{4,3},{5,2},{6,9},{7,8},{8,7},{9,6},{1... | collective-permute-start | bytes 811016 | tf_op jit(solution)/shard_map/ppermute | solution.py:305
  21.3 7.2 %collective-permute-start.2 = (bf16[33,32,128]{2,1,0:T(8,128)(2,1)S(1)}, bf16[33,32,128]{2,1,0:T(8,128)(2,1)S(1)}, u32[]{:S(2)}, u32[]{:S(2)}) collective-permute-start(bf16[33,32,128]{2,1,0:T(8,128)(2,1)S(1)} %add_convert_fusion.1.rest_0_), channel_id=1, source_target_pairs={{0,2},{1,3},{2,0},{3,1},{4,6},{5,7},{6,4},{7,5},{8,10},{9,11},{10,... | collective-permute-start | bytes 811016 | tf_op jit(solution)/shard_map/ppermute | solution.py:305
  21.4 14.1 %copy-start.3 = (bf16[33,32,128]{2,1,0:T(8,128)(2,1)}, bf16[33,32,128]{2,1,0:T(8,128)(2,1)S(1)}, u32[]{:S(2)}) copy-start(bf16[33,32,128]{2,1,0:T(8,128)(2,1)S(1)} %add_convert_fusion.rest_1_) | copy-start | bytes 811012
  21.4 14.1 %collective-permute-start.5 = (bf16[33,32,128]{2,1,0:T(8,128)(2,1)S(1)}, bf16[33,32,128]{2,1,0:T(8,128)(2,1)S(1)}, u32[]{:S(2)}, u32[]{:S(2)}) collective-permute-start(bf16[33,32,128]{2,1,0:T(8,128)(2,1)S(1)} %add_convert_fusion.rest_1_), channel_id=1, source_target_pairs={{0,127},{1,126},{2,5},{3,4},{4,3},{5,2},{6,9},{7,8},{8,7},{9,6},{1... | collective-permute-start | bytes 811016 | tf_op jit(solution)/shard_map/ppermute | solution.py:305
  27.1 8.4 %collective-permute-start.3 = (bf16[33,32,128]{2,1,0:T(8,128)(2,1)S(1)}, bf16[33,32,128]{2,1,0:T(8,128)(2,1)S(1)}, u32[]{:S(2)}, u32[]{:S(2)}) collective-permute-start(bf16[33,32,128]{2,1,0:T(8,128)(2,1)S(1)} %add_convert_fusion.rest_1_), channel_id=1, source_target_pairs={{0,2},{1,3},{2,0},{3,1},{4,6},{5,7},{6,4},{7,5},{8,10},{9,11},{10,... | collective-permute-start | bytes 811016 | tf_op jit(solution)/shard_map/ppermute | solution.py:305
  28.5 7.0 %copy-start.4 = (bf16[33,32,128]{2,1,0:T(8,128)(2,1)}, bf16[33,32,128]{2,1,0:T(8,128)(2,1)S(1)}, u32[]{:S(2)}) copy-start(bf16[33,32,128]{2,1,0:T(8,128)(2,1)S(1)} %collective-permute-done.4.rest_4_) | copy-start | bytes 811012
  28.5 7.0 %copy-start.5 = (bf16[33,32,128]{2,1,0:T(8,128)(2,1)}, bf16[33,32,128]{2,1,0:T(8,128)(2,1)S(1)}, u32[]{:S(2)}) copy-start(bf16[33,32,128]{2,1,0:T(8,128)(2,1)S(1)} %collective-permute-done.2.rest_2_) | copy-start | bytes 811012
  35.5 0.7 %copy-start.6 = (bf16[33,32,128]{2,1,0:T(8,128)(2,1)}, bf16[33,32,128]{2,1,0:T(8,128)(2,1)S(1)}, u32[]{:S(2)}) copy-start(bf16[33,32,128]{2,1,0:T(8,128)(2,1)S(1)} %collective-permute-done.5.rest_5_) | copy-start | bytes 811012
  36.2 0.7 %copy-start.7 = (bf16[33,32,128]{2,1,0:T(8,128)(2,1)}, bf16[33,32,128]{2,1,0:T(8,128)(2,1)S(1)}, u32[]{:S(2)}) copy-start(bf16[33,32,128]{2,1,0:T(8,128)(2,1)S(1)} %collective-permute-done.3.rest_3_) | copy-start | bytes 811012

commit v4 on v3

--- a/solution.py
+++ b/solution.py
@@ -25,47 +25,66 @@
     return jnp.where(iota((HALF, N), 1) >= iota((HALF, N), 0), top, bottom)
 
 
-def gram_kernel(step, first, count_ref, y_ref, d_ref, out_ref, diag_ref, proj_ref):
-    slots = y_ref.shape[1]
-    total = diag_ref.shape[0]
-    base = pl.program_id(0) * step
+def gram_kernel(step, first, count_hbm, y_hbm, d_hbm, out_ref, count_ref, y_ref, d_ref, diag_ref, proj_ref,
+                y_sems, sems):
+    total, slots = y_ref.shape[:2]
+    small = [
+        pltpu.make_async_copy(count_hbm, count_ref, sems.at[0]),
+        pltpu.make_async_copy(d_hbm.at[pl.ds(first, total)], d_ref, sems.at[1]),
+    ]
+
+    def fetch(r):
+        return pltpu.make_async_copy(y_hbm.at[first + r], y_ref.at[r], y_sems.at[r])
+
+    small[0].start()
+    fetch(0).start()
+    small[1].start()
+    for r in range(1, total):
+        fetch(r).start()
+    small[0].wait()
+    small[1].wait()
+    base = lax.axis_index("obs") * slots
     rows = lax.broadcasted_iota(jnp.int16, (slots, N), 0)
     on_ridge = iota((HALF, N), 0) + HALF == iota((HALF, N), 1)
-    start = pl.multiple_of((base // 16) * 16, 16)
-    drows = iota((16, N), 0)
-    d = d_ref[pl.ds(pl.multiple_of(first + start, 16), 16), :]
-    for s in range(step):
-        r = base + s
-        live = jnp.clip(count_ref[first + r] - lax.axis_index("obs") * slots, 0, slots).astype(jnp.int16)
-        y = jnp.where(rows < live, y_ref[s], jnp.zeros((), BF16))
-        full = jnp.dot(jnp.concatenate([y.T, d], axis=0), y, preferred_element_type=F32)
-        packed = pack(full[:N]).astype(BF16)
-        out_ref[2 * r] = packed[:HALF // 2]
-        out_ref[2 * r + 1] = packed[HALF // 2:]
-        diag_ref[pl.ds(r, 1), :] = jnp.sum(jnp.where(on_ridge, full[HALF:N], 0.0), axis=0, keepdims=True)
-        proj_ref[pl.ds(r, 1), :] = jnp.sum(jnp.where(drows == r - start, full[N:], 0.0), axis=0, keepdims=True)
-
-    @pl.when(pl.program_id(0) == pl.num_programs(0) - 1)
-    def _():
-        out_ref[2 * total] = jnp.concatenate([diag_ref[...], proj_ref[...]], axis=0).astype(BF16)
+    drows = iota((total, N), 0)
+
+    def some(t, _):
+        for s in range(step):
+            fetch(t * step + s).wait()
+        for s in range(step):
+            r = t * step + s
+            live = jnp.clip(count_ref[first + r] - base, 0, slots).astype(jnp.int16)
+            y = jnp.where(rows < live, y_ref[r], jnp.zeros((), BF16))
+            full = jnp.dot(jnp.concatenate([y.T, d_ref[...]], axis=0), y, preferred_element_type=F32)
+            packed = pack(full[:N]).astype(BF16)
+            out_ref[2 * r] = packed[:HALF // 2]
+            out_ref[2 * r + 1] = packed[HALF // 2:]
+            diag_ref[pl.ds(r, 1), :] = jnp.sum(jnp.where(on_ridge, full[HALF:N], 0.0), axis=0, keepdims=True)
+            proj_ref[pl.ds(r, 1), :] = jnp.sum(jnp.where(drows == r, full[N:], 0.0), axis=0, keepdims=True)
+        return 0
+
+    lax.fori_loop(0, total // step, some, 0)
+    out_ref[2 * total] = jnp.concatenate([diag_ref[...], proj_ref[...]], axis=0).astype(BF16)
 
 
 def grams(obs_count, obs_anomaly, innovation, first, step=8):
     regions, slots, _ = obs_anomaly.shape
+    hbm = pl.BlockSpec(memory_space=pltpu.HBM)
     return pl.pallas_call(
         functools.partial(gram_kernel, step, first),
         out_shape=jax.ShapeDtypeStruct((2 * CHUNK + 1, HALF // 2, N), BF16),
-        grid_spec=pltpu.PrefetchScalarGridSpec(
-            num_scalar_prefetch=1,
-            grid=(CHUNK // step,),
-            in_specs=[
-                pl.BlockSpec((step, slots, N), lambda i, c: (i + first // step, 0, 0)),
-                pl.BlockSpec((regions, slots), lambda i, c: (0, 0)),
-            ],
-            out_specs=pl.BlockSpec((2 * CHUNK + 1, HALF // 2, N), lambda i, c: (0, 0, 0)),
-            scratch_shapes=[pltpu.VMEM((CHUNK, N), F32), pltpu.VMEM((CHUNK, N), F32)],
-        ),
-        compiler_params=pltpu.CompilerParams(vmem_limit_bytes=48 << 20),
+        in_specs=[hbm, hbm, hbm],
+        out_specs=pl.BlockSpec(memory_space=pltpu.VMEM),
+        scratch_shapes=[
+            pltpu.SMEM((regions,), jnp.int32),
+            pltpu.VMEM((CHUNK, slots, N), BF16),
+            pltpu.VMEM((CHUNK, slots), BF16),
+            pltpu.VMEM((CHUNK, N), F32),
+            pltpu.VMEM((CHUNK, N), F32),
+            pltpu.SemaphoreType.DMA((CHUNK,)),
+            pltpu.SemaphoreType.DMA((2,)),
+        ],
+        compiler_params=pltpu.CompilerParams(vmem_limit_bytes=63 << 20),
         name="grams",
     )(obs_count, obs_anomaly, innovation)
 
@@ -166,22 +185,14 @@
 def update_kernel(idx_ref, taper_ref, idxv_ref, taperv_ref, pmean_ref, param_ref, *rest):
     chunks = idxv_ref.shape[0] // CHUNK
     parts, rest = rest[:3 * chunks], rest[3 * chunks:]
-    (out_ref, wide_ref, mat_ref, small_ref, z_ref, diag_ref, mean_ref, held_ref, made_ref, sems,
+    (out_ref, wide_ref, mat_ref, small_ref, z_ref, diag_ref, mean_ref, held_ref, made_ref,
      held_sem, made_sems) = rest
     regions, nb = idxv_ref.shape
-    ends = 2 * 3 * regions
-    copies = []
+    held = pltpu.make_async_copy(param_ref, held_ref, held_sem)
+    held.start()
     for s, src in enumerate(parts):
-        copies.append(pltpu.make_async_copy(
-            src.at[pl.ds(0, 2 * CHUNK)], wide_ref.at[pl.ds(s * 2 * CHUNK, 2 * CHUNK)], sems.at[2 * s]))
-        copies.append(pltpu.make_async_copy(src.at[2 * CHUNK], wide_ref.at[ends + s], sems.at[2 * s + 1]))
-    held = pltpu.make_async_copy(param_ref, held_ref, held_sem)
-    for c in copies:
-        c.start()
-    held.start()
-    for c in copies:
-        c.wait()
-    tails = [wide_ref[ends + s].astype(F32) for s in range(3 * chunks)]
+        wide_ref[pl.ds(s * 2 * CHUNK, 2 * CHUNK)] = src[pl.ds(0, 2 * CHUNK)]
+    tails = [src[2 * CHUNK].astype(F32) for src in parts]
     sel_lane = iota((regions, 3 * regions), 1)
     weights = jnp.zeros((regions, 3 * regions), F32)
     for k in range(nb):
@@ -273,10 +284,10 @@
     return pl.pallas_call(
         update_kernel,
         out_shape=jax.ShapeDtypeStruct(param_anomaly.shape, BF16),
-        in_specs=[smem, smem, vmem, vmem, vmem, hbm] + [hbm] * len(parts),
+        in_specs=[smem, smem, vmem, vmem, vmem, hbm] + [vmem] * len(parts),
         out_specs=hbm,
         scratch_shapes=[
-            pltpu.VMEM((6 * regions + len(parts), HALF // 2, N), BF16),
+            pltpu.VMEM((6 * regions, HALF // 2, N), BF16),
             pltpu.VMEM((regions * N, N), F32),
             pltpu.VMEM((regions * 2 * BLK, N), F32),
             pltpu.VMEM((regions * BLK, N), F32),
@@ -284,11 +295,10 @@
             pltpu.VMEM((regions, N), F32),
             pltpu.VMEM(param_anomaly.shape, BF16),
             pltpu.VMEM(param_anomaly.shape, BF16),
-            pltpu.SemaphoreType.DMA((2 * len(parts),)),
             pltpu.SemaphoreType.DMA,
             pltpu.SemaphoreType.DMA((regions,)),
         ],
-        compiler_params=pltpu.CompilerParams(vmem_limit_bytes=56 << 20),
+        compiler_params=pltpu.CompilerParams(vmem_limit_bytes=48 << 20),
         name="solve_update",
     )(idx, taper, idx, taper, param_mean, param_anomaly, *parts)
 

time: 59.9 us -> 59.7 us (level)
  local copies, waits for them, and re-layouts: 3.67 us -> 2.39 us
    pallas_call x1, Pallas kernels: 22.6 us -> 21.2 us  [solve_update(): pl.pallas_call(update_kernel, out_shape=jax.ShapeDtypeStruct(param_anomal...]
    pallas_call x2, Pallas kernels: 7.96 us -> 9.35 us  [grams(): pl.pallas_call(functools.partial(gram_kernel, step, first), out_shape=jax...]
    unnamed x22 -> x12, local copies, waits for them, and re-layouts: 3.67 us -> 2.39 us
    convert_element_type x2, other arithmetic: 0.15 us -> 1.11 us  [body(): both = (packed.astype(F32) + partner.astype(F32)).astype(BF16)]
  transfers between devices with their start and end apart: 6 -> 6, of which waited for: 2 -> 2; matrix products, arithmetic and copies ran while one was open for 3% -> 2% of each run, Pallas kernels for 7% -> 8%
where the time goes in v4:
time: 59.7 us; the launch traced here: 59.5 us
  Pallas kernels  30.6 us (51%)
  starting transfers between devices  15.3 us (26%)
  waiting for transfers between devices  9.79 us (16%)
  local copies, waits for them, and re-layouts  2.39 us (4%)
  other arithmetic  1.14 us (2%)
    pallas_call x1, Pallas kernels, solve_update(): pl.pallas_call(update_kernel, out_shape=jax.ShapeDtypeStruct(param_anomal...  21.2 us
    ppermute x6, starting transfers between devices, swap(): return lax.ppermute(x, ('region', 'obs'), line)  15.3 us
    ppermute x6, waiting for transfers between devices, swap(): return lax.ppermute(x, ('region', 'obs'), line)  9.79 us
    pallas_call x2, Pallas kernels, grams(): pl.pallas_call(functools.partial(gram_kernel, step, first), out_shape=jax...  9.35 us
    unnamed x12, local copies, waits for them, and re-layouts  2.39 us
  transfers between devices with their start and end apart: 6, of which 2 were waited for; matrix products, arithmetic and copies ran while one was open for 2% of the time, Pallas kernels for 8%

profile of v4, /device:TPU:0, one launch (start us, length us, event | category | flops | bytes accessed | tf_op | source)
XLA Modules:
  0.0 59.5 jit_solution(844146912640504705)
XLA Ops:
  0.0 4.7 %grams.2 = bf16[33,32,128]{2,1,0:T(8,128)(2,1)} custom-call(s32[32]{0:T(128)} %count_hbm.3, bf16[32,1024,128]{2,1,0:T(8,128)(2,1)} %y_hbm.3, bf16[32,1024]{1,0:T(8,128)(2,1)} %d_hbm.3), custom_call_target="tpu_custom_call" | custom-call | tf_op jit(solution)/shard_map/grams/pallas_call | solution.py:73
  4.7 0.0 copy-start.2
  4.7 0.0 copy-start.3
  4.7 0.0 copy-start.4
  4.7 0.0 copy-start.1
  4.7 1.7 %collective-permute-start = (bf16[33,32,128]{2,1,0:T(8,128)(2,1)}, bf16[33,32,128]{2,1,0:T(8,128)(2,1)S(1)}, u32[]{:S(2)}, u32[]{:S(2)}) collective-permute-start(bf16[33,32,128]{2,1,0:T(8,128)(2,1)} %grams.2), channel_id=1, source_target_pairs={{0,1},{1,0},{2,3},{3,2},{4,5},{5,4},{6,7},{7,6},{8,9},{9,8},{10,11... | collective-permute-start | bytes 811016 | tf_op jit(solution)/shard_map/ppermute | solution.py:315
  6.4 4.7 %grams.3 = bf16[33,32,128]{2,1,0:T(8,128)(2,1)} custom-call(s32[32]{0:T(128)} %count_hbm.3, bf16[32,1024,128]{2,1,0:T(8,128)(2,1)} %y_hbm.3, bf16[32,1024]{1,0:T(8,128)(2,1)} %d_hbm.3), custom_call_target="tpu_custom_call" | custom-call | tf_op jit(solution)/shard_map/grams/pallas_call | solution.py:73
  11.1 0.5 collective-permute-start.1
  11.6 1.8 %collective-permute-done = bf16[33,32,128]{2,1,0:T(8,128)(2,1)S(1)} collective-permute-done((bf16[33,32,128]{2,1,0:T(8,128)(2,1)}, bf16[33,32,128]{2,1,0:T(8,128)(2,1)S(1)}, u32[]{:S(2)}, u32[]{:S(2)}) %collective-permute-start) | collective-permute-done | bytes 270368 | tf_op jit(solution)/shard_map/ppermute | solution.py:315
  13.4 0.0 copy-done.2
  13.4 0.1 add_convert_fusion.1.rest_0_
  13.4 7.3 %collective-permute-start.4 = (bf16[33,32,128]{2,1,0:T(8,128)(2,1)S(1)}, bf16[33,32,128]{2,1,0:T(8,128)(2,1)S(1)}, u32[]{:S(2)}, u32[]{:S(2)}) collective-permute-start(bf16[33,32,128]{2,1,0:T(8,128)(2,1)S(1)} %add_convert_fusion.1.rest_0_), channel_id=1, source_target_pairs={{0,127},{1,126},{2,5},{3,4},{4,3},{5,2},{6,9},{7,8},{8,7},{9,6},{1... | collective-permute-start | bytes 811016 | tf_op jit(solution)/shard_map/ppermute | solution.py:315
  20.7 0.0 collective-permute-start.2
  20.7 0.0 collective-permute-done.1
  20.7 1.0 %add_convert_fusion.rest_1_ = bf16[33,32,128]{2,1,0:T(8,128)(2,1)S(1)} fusion(bf16[33,32,128]{2,1,0:T(8,128)(2,1)S(1)} %collective-permute-done.1, bf16[33,32,128]{2,1,0:T(8,128)(2,1)} %grams.3), kind=kLoop, calls=%fused_computation | loop fusion | flops 540672 | bytes 811008 | tf_op jit(solution)/shard_map/convert_element_type | solution.py:321
  21.8 5.9 %collective-permute-start.5 = (bf16[33,32,128]{2,1,0:T(8,128)(2,1)S(1)}, bf16[33,32,128]{2,1,0:T(8,128)(2,1)S(1)}, u32[]{:S(2)}, u32[]{:S(2)}) collective-permute-start(bf16[33,32,128]{2,1,0:T(8,128)(2,1)S(1)} %add_convert_fusion.rest_1_), channel_id=1, source_target_pairs={{0,127},{1,126},{2,5},{3,4},{4,3},{5,2},{6,9},{7,8},{8,7},{9,6},{1... | collective-permute-start | bytes 811016 | tf_op jit(solution)/shard_map/ppermute | solution.py:315
  27.6 0.0 collective-permute-start.3
  27.6 0.0 copy-done.3
  27.6 0.1 copy.8
  27.7 0.0 copy-done.4
  27.7 0.1 copy.9.taper_ref.taperv_ref
  27.8 0.0 collective-permute-done.4.rest_4_
  27.9 0.0 collective-permute-done.2.rest_2_
  27.9 8.0 %collective-permute-done.5.rest_5_ = bf16[33,32,128]{2,1,0:T(8,128)(2,1)S(1)} collective-permute-done((bf16[33,32,128]{2,1,0:T(8,128)(2,1)S(1)}, bf16[33,32,128]{2,1,0:T(8,128)(2,1)S(1)}, u32[]{:S(2)}, u32[]{:S(2)}) %collective-permute-start.5) | collective-permute-done | bytes 270368 | tf_op jit(solution)/shard_map/ppermute | solution.py:315
  35.9 0.0 collective-permute-done.3.rest_3_
  35.9 0.0 copy-done.1
  35.9 0.0 copy-start
  35.9 2.2 %copy-done = bf16[32,512,128]{2,1,0:T(8,128)(2,1)S(1)} copy-done((bf16[32,512,128]{2,1,0:T(8,128)(2,1)S(1)}, bf16[32,512,128]{2,1,0:T(8,128)(2,1)}, u32[]{:S(2)}) %copy-start) | copy-done | bytes 4194328
  38.1 21.2 %solve_update.1 = bf16[32,512,128]{2,1,0:T(8,128)(2,1)} custom-call(s32[32,5]{1,0:T(8,128)S(1)} %fusion.2.idx_ref.idxv_ref, f32[32,5]{1,0:T(8,128)S(1)} %copy.9.taper_ref.taperv_ref, s32[32,5]{1,0:T(8,128)S(1)} %fusion.2.idx_ref.idxv_ref, f32[32,5]{1,0:T(8,128)S(1)} %copy.9.taper_ref.taperv_ref, f32[32,512]{1,0:T(8,128)S(1)} %copy-done.1, ...), custom_call_target="tpu_custom_call" | custom-call | tf_op jit(solution)/shard_map/solve_update/pallas_call | solution.py:284
  (1 shorter events, 0.0 us)
Async XLA Ops:
  4.7 8.7 %copy-start.2 = (bf16[33,32,128]{2,1,0:T(8,128)(2,1)S(1)}, bf16[33,32,128]{2,1,0:T(8,128)(2,1)}, u32[]{:S(2)}) copy-start(bf16[33,32,128]{2,1,0:T(8,128)(2,1)} %grams.2) | copy-start | bytes 811012
  4.7 22.9 %copy-start.3 = (s32[32,5]{0,1:T(8,128)S(1)}, s32[32,5]{0,1:T(8,128)}, u32[]{:S(2)}) copy-start(s32[32,5]{0,1:T(8,128)} %param.10) | copy-start | bytes 1924
  4.7 23.0 %copy-start.4 = (f32[32,5]{0,1:T(8,128)S(1)}, f32[32,5]{0,1:T(8,128)}, u32[]{:S(2)}) copy-start(f32[32,5]{0,1:T(8,128)} %param.11) | copy-start | bytes 1924
  4.7 31.2 %copy-start.1 = (f32[32,512]{1,0:T(8,128)S(1)}, f32[32,512]{1,0:T(8,128)}, u32[]{:S(2)}) copy-start(f32[32,512]{1,0:T(8,128)} %pmean_ref.1) | copy-start | bytes 196612
  4.7 8.6 %collective-permute-start = (bf16[33,32,128]{2,1,0:T(8,128)(2,1)}, bf16[33,32,128]{2,1,0:T(8,128)(2,1)S(1)}, u32[]{:S(2)}, u32[]{:S(2)}) collective-permute-start(bf16[33,32,128]{2,1,0:T(8,128)(2,1)} %grams.2), channel_id=1, source_target_pairs={{0,1},{1,0},{2,3},{3,2},{4,5},{5,4},{6,7},{7,6},{8,9},{9,8},{10,11... | collective-permute-start | bytes 811016 | tf_op jit(solution)/shard_map/ppermute | solution.py:315
  11.1 9.7 %collective-permute-start.1 = (bf16[33,32,128]{2,1,0:T(8,128)(2,1)}, bf16[33,32,128]{2,1,0:T(8,128)(2,1)S(1)}, u32[]{:S(2)}, u32[]{:S(2)}) collective-permute-start(bf16[33,32,128]{2,1,0:T(8,128)(2,1)} %grams.3), channel_id=1, source_target_pairs={{0,1},{1,0},{2,3},{3,2},{4,5},{5,4},{6,7},{7,6},{8,9},{9,8},{10,11... | collective-permute-start | bytes 811016 | tf_op jit(solution)/shard_map/ppermute | solution.py:315
  13.4 14.4 %collective-permute-start.4 = (bf16[33,32,128]{2,1,0:T(8,128)(2,1)S(1)}, bf16[33,32,128]{2,1,0:T(8,128)(2,1)S(1)}, u32[]{:S(2)}, u32[]{:S(2)}) collective-permute-start(bf16[33,32,128]{2,1,0:T(8,128)(2,1)S(1)} %add_convert_fusion.1.rest_0_), channel_id=1, source_target_pairs={{0,127},{1,126},{2,5},{3,4},{4,3},{5,2},{6,9},{7,8},{8,7},{9,6},{1... | collective-permute-start | bytes 811016 | tf_op jit(solution)/shard_map/ppermute | solution.py:315
  20.7 7.1 %collective-permute-start.2 = (bf16[33,32,128]{2,1,0:T(8,128)(2,1)S(1)}, bf16[33,32,128]{2,1,0:T(8,128)(2,1)S(1)}, u32[]{:S(2)}, u32[]{:S(2)}) collective-permute-start(bf16[33,32,128]{2,1,0:T(8,128)(2,1)S(1)} %add_convert_fusion.1.rest_0_), channel_id=1, source_target_pairs={{0,2},{1,3},{2,0},{3,1},{4,6},{5,7},{6,4},{7,5},{8,10},{9,11},{10,... | collective-permute-start | bytes 811016 | tf_op jit(solution)/shard_map/ppermute | solution.py:315
  21.8 14.1 %collective-permute-start.5 = (bf16[33,32,128]{2,1,0:T(8,128)(2,1)S(1)}, bf16[33,32,128]{2,1,0:T(8,128)(2,1)S(1)}, u32[]{:S(2)}, u32[]{:S(2)}) collective-permute-start(bf16[33,32,128]{2,1,0:T(8,128)(2,1)S(1)} %add_convert_fusion.rest_1_), channel_id=1, source_target_pairs={{0,127},{1,126},{2,5},{3,4},{4,3},{5,2},{6,9},{7,8},{8,7},{9,6},{1... | collective-permute-start | bytes 811016 | tf_op jit(solution)/shard_map/ppermute | solution.py:315
  27.6 8.3 %collective-permute-start.3 = (bf16[33,32,128]{2,1,0:T(8,128)(2,1)S(1)}, bf16[33,32,128]{2,1,0:T(8,128)(2,1)S(1)}, u32[]{:S(2)}, u32[]{:S(2)}) collective-permute-start(bf16[33,32,128]{2,1,0:T(8,128)(2,1)S(1)} %add_convert_fusion.rest_1_), channel_id=1, source_target_pairs={{0,2},{1,3},{2,0},{3,1},{4,6},{5,7},{6,4},{7,5},{8,10},{9,11},{10,... | collective-permute-start | bytes 811016 | tf_op jit(solution)/shard_map/ppermute | solution.py:315
  35.9 2.2 %copy-start = (bf16[32,512,128]{2,1,0:T(8,128)(2,1)S(1)}, bf16[32,512,128]{2,1,0:T(8,128)(2,1)}, u32[]{:S(2)}) copy-start(bf16[32,512,128]{2,1,0:T(8,128)(2,1)} %param_ref.1) | copy-start | bytes 12582916

commit v5 on v4

--- a/solution.py
+++ b/solution.py
@@ -11,7 +11,7 @@
 HALF = 64
 CHUNK = 16
 BLK = 16
-U1, U2, U3 = 32, 32, 8
+U3 = 8
 F32 = jnp.float32
 BF16 = jnp.bfloat16
 
@@ -110,11 +110,11 @@
         mat_ref[pl.ds(row + HALF, HALF), :] = jnp.where(j < HALF, tl, corner)
 
 
-def factor(mat_ref, small_ref, regions, kb):
+def factor(mat_ref, small_ref, begin, regions, kb):
     sub = iota((BLK, regions), 0)
     x = []
     for i in range(BLK):
-        row = mat_ref[pl.ds(kb + i, regions, stride=N), :]
+        row = mat_ref[pl.ds(begin * N + kb + i, regions, stride=N), :]
         x.append(row.T[kb:kb + BLK])
     lower = []
     for i in range(BLK):
@@ -123,33 +123,55 @@
         for j in range(i + 1, BLK):
             x[j] = jnp.where(sub == i, 0.0, x[j]) - (x[i][j:j + 1] * scale) * r
         lower.append(jnp.where(sub <= i, r, 0.0))
+        yield
     inverse = []
     for a in range(BLK):
         z = lower[a][a:a + 1] * lower[a]
         for i in range(a + 1, BLK):
             z = z + lower[i][a:a + 1] * lower[i]
         inverse.append(z)
+        if a % 2:
+            yield
     per = N // BLK
     lane = iota((regions, N), 1)
     for start, block in ((0, lower), (BLK, inverse)):
         for part in range(BLK // per):
             turned = jnp.concatenate(block[part * per:(part + 1) * per], axis=0).T
+            yield
             for q in range(per):
                 row = jnp.where((lane >= q * BLK) & (lane < (q + 1) * BLK), turned, 0.0)
-                small_ref[pl.ds(start + part * per + q, regions, stride=2 * BLK), :] = row
+                small_ref[pl.ds(begin * 2 * BLK + start + part * per + q, regions, stride=2 * BLK), :] = row
+
+
+def products(mat_ref, small_ref, z_ref, begin, regions, kb):
+    for m in range(begin, begin + regions):
+        reduce_rows(mat_ref, small_ref, z_ref, m, kb)
+        yield
+    if kb + BLK < N:
+        for m in range(begin, begin + regions):
+            update(mat_ref, z_ref, m, kb)
+            yield
+
+
+def beside(one, other):
+    live = [one, other]
+    while live:
+        for part in list(live):
+            if next(part, live) is live:
+                live.remove(part)
 
 
 def reduce_rows(mat_ref, small_ref, z_ref, m, kb):
-    start = pl.multiple_of(m * N + kb, BLK)
+    start = m * N + kb
     rows = mat_ref[pl.ds(start, BLK), :]
     lane, sub = iota((BLK, N), 1), iota((BLK, N), 0)
     inside = (lane >= kb) & (lane < kb + BLK)
     rows = jnp.where(inside, jnp.where(lane - kb == sub, 1.0, 0.0), rows)
     rh, rl = split(rows)
-    sh, sl = split(small_ref[pl.ds(pl.multiple_of(m * 2 * BLK, 2 * BLK), 2 * BLK), :])
+    sh, sl = split(small_ref[pl.ds(m * 2 * BLK, 2 * BLK), :])
     both = mul_m(sh, sl, jnp.concatenate([rh] * (N // BLK), axis=0), jnp.concatenate([rl] * (N // BLK), axis=0))
     mat_ref[pl.ds(start, BLK), :] = jnp.where(lane < kb + BLK, both[:BLK], 0.0)
-    z_ref[pl.ds(pl.multiple_of(m * BLK, BLK), BLK), :] = both[BLK:]
+    z_ref[pl.ds(m * BLK, BLK), :] = both[BLK:]
 
 
 def mul_k(ah, al, bh, bl):
@@ -167,10 +189,10 @@
 
 def update(mat_ref, z_ref, m, kb):
     n = N - kb - BLK
-    start = pl.multiple_of(m * N + kb + BLK, BLK)
+    start = m * N + kb + BLK
     mat = mat_ref[pl.ds(start, n), :]
     high, low = split(mat)
-    zh, zl = split(z_ref[pl.ds(pl.multiple_of(m * BLK, BLK), BLK), :])
+    zh, zl = split(z_ref[pl.ds(m * BLK, BLK), :])
     above, below = jnp.zeros((kb, N), BF16), jnp.zeros((n, N), BF16)
 
     def place(z):
@@ -217,22 +239,14 @@
         return 0
 
     lax.fori_loop(0, regions // 2, combine, 0, unroll=8)
+    count = regions // 2
+    before = iter(())
     for kb in range(0, N, BLK):
-        factor(mat_ref, small_ref, regions, kb)
-
-        def first(t, _, kb=kb):
-            for u in range(U1):
-                reduce_rows(mat_ref, small_ref, z_ref, t * U1 + u, kb)
-            return 0
-
-        def second(t, _, kb=kb):
-            for u in range(U2):
-                update(mat_ref, z_ref, t * U2 + u, kb)
-            return 0
-
-        lax.fori_loop(0, regions // U1, first, 0)
-        if kb + BLK < N:
-            lax.fori_loop(0, regions // U2, second, 0)
+        for begin in (0, count):
+            beside(factor(mat_ref, small_ref, begin, count, kb), before)
+            before = products(mat_ref, small_ref, z_ref, begin, count, kb)
+    for _ in before:
+        pass
 
     def weigh(t, mean):
         for u in range(32):
@@ -298,7 +312,7 @@
             pltpu.SemaphoreType.DMA,
             pltpu.SemaphoreType.DMA((regions,)),
         ],
-        compiler_params=pltpu.CompilerParams(vmem_limit_bytes=48 << 20),
+        compiler_params=pltpu.CompilerParams(vmem_limit_bytes=50 << 20),
         name="solve_update",
     )(idx, taper, idx, taper, param_mean, param_anomaly, *parts)
 

time: 59.7 us -> 56.8 us (0.951)
  local copies, waits for them, and re-layouts: 2.39 us -> 0.2 us
  Pallas kernels: 30.6 us -> 29.9 us
    unnamed x12 -> x10, local copies, waits for them, and re-layouts: 2.39 us -> 0.2 us
    pallas_call x1, Pallas kernels: 21.2 us -> 20.6 us  [solve_update(): pl.pallas_call(update_kernel, out_shape=jax.ShapeDtypeStruct(param_anomal...]
where the time goes in v5:
time: 56.8 us; the launch traced here: 56.6 us
  Pallas kernels  29.9 us (53%)
  starting transfers between devices  15.3 us (27%)
  waiting for transfers between devices  9.79 us (17%)
  other arithmetic  1.14 us (2%)
    pallas_call x1, Pallas kernels, solve_update(): pl.pallas_call(update_kernel, out_shape=jax.ShapeDtypeStruct(param_anomal...  20.6 us
    ppermute x6, starting transfers between devices, swap(): return lax.ppermute(x, ('region', 'obs'), line)  15.3 us
    ppermute x6, waiting for transfers between devices, swap(): return lax.ppermute(x, ('region', 'obs'), line)  9.79 us
    pallas_call x2, Pallas kernels, grams(): pl.pallas_call(functools.partial(gram_kernel, step, first), out_shape=jax...  9.35 us
  transfers between devices with their start and end apart: 6, of which 2 were waited for; matrix products, arithmetic and copies ran while one was open for 2% of the time, Pallas kernels for 8%

profile of v5, /device:TPU:0, one launch (start us, length us, event | category | flops | bytes accessed | tf_op | source)
XLA Modules:
  0.0 56.6 jit_solution(8815446419359765987)
XLA Ops:
  0.0 4.7 %grams.2 = bf16[33,32,128]{2,1,0:T(8,128)(2,1)} custom-call(s32[32]{0:T(128)} %count_hbm.3, bf16[32,1024,128]{2,1,0:T(8,128)(2,1)} %y_hbm.3, bf16[32,1024]{1,0:T(8,128)(2,1)} %d_hbm.3), custom_call_target="tpu_custom_call" | custom-call | tf_op jit(solution)/shard_map/grams/pallas_call | solution.py:73
  4.7 0.0 copy-start.1
  4.7 0.0 copy-start.2
  4.7 0.0 copy-start.3
  4.7 0.0 copy-start
  4.7 1.7 %collective-permute-start = (bf16[33,32,128]{2,1,0:T(8,128)(2,1)}, bf16[33,32,128]{2,1,0:T(8,128)(2,1)S(1)}, u32[]{:S(2)}, u32[]{:S(2)}) collective-permute-start(bf16[33,32,128]{2,1,0:T(8,128)(2,1)} %grams.2), channel_id=1, source_target_pairs={{0,1},{1,0},{2,3},{3,2},{4,5},{5,4},{6,7},{7,6},{8,9},{9,8},{10,11... | collective-permute-start | bytes 811016 | tf_op jit(solution)/shard_map/ppermute | solution.py:329
  6.4 4.7 %grams.3 = bf16[33,32,128]{2,1,0:T(8,128)(2,1)} custom-call(s32[32]{0:T(128)} %count_hbm.3, bf16[32,1024,128]{2,1,0:T(8,128)(2,1)} %y_hbm.3, bf16[32,1024]{1,0:T(8,128)(2,1)} %d_hbm.3), custom_call_target="tpu_custom_call" | custom-call | tf_op jit(solution)/shard_map/grams/pallas_call | solution.py:73
  11.1 0.5 collective-permute-start.1
  11.6 1.7 %collective-permute-done = bf16[33,32,128]{2,1,0:T(8,128)(2,1)S(1)} collective-permute-done((bf16[33,32,128]{2,1,0:T(8,128)(2,1)}, bf16[33,32,128]{2,1,0:T(8,128)(2,1)S(1)}, u32[]{:S(2)}, u32[]{:S(2)}) %collective-permute-start) | collective-permute-done | bytes 270368 | tf_op jit(solution)/shard_map/ppermute | solution.py:329
  13.3 0.0 copy-done.1
  13.3 0.1 add_convert_fusion.1.rest_0_
  13.4 7.3 %collective-permute-start.4 = (bf16[33,32,128]{2,1,0:T(8,128)(2,1)S(1)}, bf16[33,32,128]{2,1,0:T(8,128)(2,1)S(1)}, u32[]{:S(2)}, u32[]{:S(2)}) collective-permute-start(bf16[33,32,128]{2,1,0:T(8,128)(2,1)S(1)} %add_convert_fusion.1.rest_0_), channel_id=1, source_target_pairs={{0,127},{1,126},{2,5},{3,4},{4,3},{5,2},{6,9},{7,8},{8,7},{9,6},{1... | collective-permute-start | bytes 811016 | tf_op jit(solution)/shard_map/ppermute | solution.py:329
  20.7 0.0 collective-permute-start.2
  20.7 0.0 collective-permute-done.1
  20.7 1.0 %add_convert_fusion.rest_1_ = bf16[33,32,128]{2,1,0:T(8,128)(2,1)S(1)} fusion(bf16[33,32,128]{2,1,0:T(8,128)(2,1)S(1)} %collective-permute-done.1, bf16[33,32,128]{2,1,0:T(8,128)(2,1)} %grams.3), kind=kLoop, calls=%fused_computation | loop fusion | flops 540672 | bytes 811008 | tf_op jit(solution)/shard_map/convert_element_type | solution.py:335
  21.8 5.8 %collective-permute-start.5 = (bf16[33,32,128]{2,1,0:T(8,128)(2,1)S(1)}, bf16[33,32,128]{2,1,0:T(8,128)(2,1)S(1)}, u32[]{:S(2)}, u32[]{:S(2)}) collective-permute-start(bf16[33,32,128]{2,1,0:T(8,128)(2,1)S(1)} %add_convert_fusion.rest_1_), channel_id=1, source_target_pairs={{0,127},{1,126},{2,5},{3,4},{4,3},{5,2},{6,9},{7,8},{8,7},{9,6},{1... | collective-permute-start | bytes 811016 | tf_op jit(solution)/shard_map/ppermute | solution.py:329
  27.6 0.0 collective-permute-start.3
  27.6 0.0 copy-done.2
  27.6 0.1 copy.8
  27.7 0.0 copy-done.3
  27.7 0.1 copy.9.taper_ref.taperv_ref
  27.8 0.0 collective-permute-done.4.rest_4_
  27.8 0.0 collective-permute-done.2.rest_2_
  27.9 8.0 %collective-permute-done.5.rest_5_ = bf16[33,32,128]{2,1,0:T(8,128)(2,1)S(1)} collective-permute-done((bf16[33,32,128]{2,1,0:T(8,128)(2,1)S(1)}, bf16[33,32,128]{2,1,0:T(8,128)(2,1)S(1)}, u32[]{:S(2)}, u32[]{:S(2)}) %collective-permute-start.5) | collective-permute-done | bytes 270368 | tf_op jit(solution)/shard_map/ppermute | solution.py:329
  35.9 0.0 collective-permute-done.3.rest_3_
  35.9 0.0 copy-done
  35.9 20.6 %solve_update.1 = bf16[32,512,128]{2,1,0:T(8,128)(2,1)} custom-call(s32[32,5]{1,0:T(8,128)S(1)} %fusion.2.idx_ref.idxv_ref, f32[32,5]{1,0:T(8,128)S(1)} %copy.9.taper_ref.taperv_ref, s32[32,5]{1,0:T(8,128)S(1)} %fusion.2.idx_ref.idxv_ref, f32[32,5]{1,0:T(8,128)S(1)} %copy.9.taper_ref.taperv_ref, f32[32,512]{1,0:T(8,128)S(1)} %copy-done, ...), custom_call_target="tpu_custom_call" | custom-call | tf_op jit(solution)/shard_map/solve_update/pallas_call | solution.py:298
  (1 shorter events, 0.0 us)
Async XLA Ops:
  4.7 8.7 %copy-start.1 = (bf16[33,32,128]{2,1,0:T(8,128)(2,1)S(1)}, bf16[33,32,128]{2,1,0:T(8,128)(2,1)}, u32[]{:S(2)}) copy-start(bf16[33,32,128]{2,1,0:T(8,128)(2,1)} %grams.2) | copy-start | bytes 811012
  4.7 22.9 %copy-start.2 = (s32[32,5]{0,1:T(8,128)S(1)}, s32[32,5]{0,1:T(8,128)}, u32[]{:S(2)}) copy-start(s32[32,5]{0,1:T(8,128)} %param.10) | copy-start | bytes 1924
  4.7 23.0 %copy-start.3 = (f32[32,5]{0,1:T(8,128)S(1)}, f32[32,5]{0,1:T(8,128)}, u32[]{:S(2)}) copy-start(f32[32,5]{0,1:T(8,128)} %param.11) | copy-start | bytes 1924
  4.7 31.2 %copy-start = (f32[32,512]{1,0:T(8,128)S(1)}, f32[32,512]{1,0:T(8,128)}, u32[]{:S(2)}) copy-start(f32[32,512]{1,0:T(8,128)} %pmean_ref.1) | copy-start | bytes 196612
  4.7 8.6 %collective-permute-start = (bf16[33,32,128]{2,1,0:T(8,128)(2,1)}, bf16[33,32,128]{2,1,0:T(8,128)(2,1)S(1)}, u32[]{:S(2)}, u32[]{:S(2)}) collective-permute-start(bf16[33,32,128]{2,1,0:T(8,128)(2,1)} %grams.2), channel_id=1, source_target_pairs={{0,1},{1,0},{2,3},{3,2},{4,5},{5,4},{6,7},{7,6},{8,9},{9,8},{10,11... | collective-permute-start | bytes 811016 | tf_op jit(solution)/shard_map/ppermute | solution.py:329
  11.1 9.7 %collective-permute-start.1 = (bf16[33,32,128]{2,1,0:T(8,128)(2,1)}, bf16[33,32,128]{2,1,0:T(8,128)(2,1)S(1)}, u32[]{:S(2)}, u32[]{:S(2)}) collective-permute-start(bf16[33,32,128]{2,1,0:T(8,128)(2,1)} %grams.3), channel_id=1, source_target_pairs={{0,1},{1,0},{2,3},{3,2},{4,5},{5,4},{6,7},{7,6},{8,9},{9,8},{10,11... | collective-permute-start | bytes 811016 | tf_op jit(solution)/shard_map/ppermute | solution.py:329
  13.4 14.4 %collective-permute-start.4 = (bf16[33,32,128]{2,1,0:T(8,128)(2,1)S(1)}, bf16[33,32,128]{2,1,0:T(8,128)(2,1)S(1)}, u32[]{:S(2)}, u32[]{:S(2)}) collective-permute-start(bf16[33,32,128]{2,1,0:T(8,128)(2,1)S(1)} %add_convert_fusion.1.rest_0_), channel_id=1, source_target_pairs={{0,127},{1,126},{2,5},{3,4},{4,3},{5,2},{6,9},{7,8},{8,7},{9,6},{1... | collective-permute-start | bytes 811016 | tf_op jit(solution)/shard_map/ppermute | solution.py:329
  20.7 7.1 %collective-permute-start.2 = (bf16[33,32,128]{2,1,0:T(8,128)(2,1)S(1)}, bf16[33,32,128]{2,1,0:T(8,128)(2,1)S(1)}, u32[]{:S(2)}, u32[]{:S(2)}) collective-permute-start(bf16[33,32,128]{2,1,0:T(8,128)(2,1)S(1)} %add_convert_fusion.1.rest_0_), channel_id=1, source_target_pairs={{0,2},{1,3},{2,0},{3,1},{4,6},{5,7},{6,4},{7,5},{8,10},{9,11},{10,... | collective-permute-start | bytes 811016 | tf_op jit(solution)/shard_map/ppermute | solution.py:329
  21.8 14.1 %collective-permute-start.5 = (bf16[33,32,128]{2,1,0:T(8,128)(2,1)S(1)}, bf16[33,32,128]{2,1,0:T(8,128)(2,1)S(1)}, u32[]{:S(2)}, u32[]{:S(2)}) collective-permute-start(bf16[33,32,128]{2,1,0:T(8,128)(2,1)S(1)} %add_convert_fusion.rest_1_), channel_id=1, source_target_pairs={{0,127},{1,126},{2,5},{3,4},{4,3},{5,2},{6,9},{7,8},{8,7},{9,6},{1... | collective-permute-start | bytes 811016 | tf_op jit(solution)/shard_map/ppermute | solution.py:329
  27.6 8.3 %collective-permute-start.3 = (bf16[33,32,128]{2,1,0:T(8,128)(2,1)S(1)}, bf16[33,32,128]{2,1,0:T(8,128)(2,1)S(1)}, u32[]{:S(2)}, u32[]{:S(2)}) collective-permute-start(bf16[33,32,128]{2,1,0:T(8,128)(2,1)S(1)} %add_convert_fusion.rest_1_), channel_id=1, source_target_pairs={{0,2},{1,3},{2,0},{3,1},{4,6},{5,7},{6,4},{7,5},{8,10},{9,11},{10,... | collective-permute-start | bytes 811016 | tf_op jit(solution)/shard_map/ppermute | solution.py:329
